TPU v7x, 128 devices: a whole 4x4x4 slice. The times are simulated.
128 devices in a mesh: gx: 8 (over x, y_lo), gy: 4 (over y_hi, core), gz: 4 (over z).
Axes of the slice: x: 4, y: 4 (y_hi: 2, y_lo: 2; y = y_hi * 2 + y_lo), z: 4, core: 2. Of those that a mesh axis runs over, the one named last changes fastest.
Arguments:
- tokens: bfloat16 [1024, 4096], P('gy', ('gz', 'gx')), may hold values from -6 to 6
- cotangent: bfloat16 [1024, 4096], P('gy', ('gz', 'gx')), may hold values from -6 to 6
- gate_weight: bfloat16 [4096, 16384], P('gz', ('gx', 'gy')), may hold values from -0.09375 to 0.09375
- up_weight: bfloat16 [4096, 16384], P('gz', ('gx', 'gy')), may hold values from -0.09375 to 0.09375
- down_weight: bfloat16 [16384, 4096], P('gx', ('gz', 'gy')), may hold values from -0.046875 to 0.046875
Outputs:
- layer_out: bfloat16 [1024, 4096], P('gy', ('gz', 'gx'))
- grad_tokens: bfloat16 [1024, 4096], P('gy', ('gz', 'gx'))
- grad_gate: float32 [4096, 16384], P('gz', ('gx', 'gy'))
- grad_up: float32 [4096, 16384], P('gz', ('gx', 'gy'))
- grad_down: float32 [16384, 4096], P('gx', ('gz', 'gy'))
All inputs are finite; a program needn't handle non-finite values.
Results may differ from a plain program's by a relative error of at most 0.0049.
Values may be sent and summed in bfloat16 or wider, within the bound.
A program may use at most 128 MiB of HBM per device.

v0:
```python
import jax
import jax.numpy as jnp
from jax import lax
from jax.sharding import PartitionSpec as P


def matmul_tn(left, right):
    return lax.dot_general(
        left, right, (((0,), (0,)), ((), ())), preferred_element_type=jnp.float32
    )


def matmul_nt(left, right):
    return lax.dot_general(
        left, right, (((1,), (1,)), ((), ())), preferred_element_type=jnp.float32
    )


def local(tokens, cotangent, gate_weight, up_weight, down_weight):
    token_cols = lax.all_gather(tokens, "gx", axis=1, tiled=True)
    gate_cols, up_cols = (
        lax.all_gather(gate_weight, "gy", axis=1, tiled=True),
        lax.all_gather(up_weight, "gy", axis=1, tiled=True),
    )
    down_cols = lax.all_gather(down_weight, "gy", axis=1, tiled=True)
    gate_part = jnp.dot(token_cols, gate_cols, preferred_element_type=jnp.float32)
    up_part = jnp.dot(token_cols, up_cols, preferred_element_type=jnp.float32)
    gate, up = (
        lax.psum_scatter(gate_part, "gz", scatter_dimension=1, tiled=True),
        lax.psum_scatter(up_part, "gz", scatter_dimension=1, tiled=True),
    )
    sigma = jax.nn.sigmoid(gate)
    swish = gate * sigma
    hidden = (swish * up).astype(jnp.bfloat16)
    hidden_cols = lax.all_gather(hidden, "gz", axis=1, tiled=True)
    out_part = jnp.dot(hidden_cols, down_cols, preferred_element_type=jnp.float32)
    layer_out = lax.psum_scatter(out_part, "gx", scatter_dimension=1, tiled=True).astype(
        jnp.bfloat16
    )
    cot_cols = lax.all_gather(cotangent, "gx", axis=1, tiled=True)
    hidden_grad_part = matmul_nt(cot_cols, down_cols)
    grad_hidden = lax.psum_scatter(hidden_grad_part, "gz", scatter_dimension=1, tiled=True)
    grad_pre_gate = (grad_hidden * up * sigma * (1.0 + gate * (1.0 - sigma))).astype(jnp.bfloat16)
    grad_pre_up = (grad_hidden * swish).astype(jnp.bfloat16)
    gate_grad_cols, up_grad_cols = (
        lax.all_gather(grad_pre_gate, "gz", axis=1, tiled=True),
        lax.all_gather(grad_pre_up, "gz", axis=1, tiled=True),
    )
    input_part = matmul_nt(gate_grad_cols, gate_cols) + matmul_nt(up_grad_cols, up_cols)
    grad_tokens = lax.psum_scatter(input_part, "gx", scatter_dimension=1, tiled=True).astype(
        jnp.bfloat16
    )
    gate_wpart = matmul_tn(token_cols, gate_grad_cols)
    up_wpart = matmul_tn(token_cols, up_grad_cols)
    grad_gate, grad_up = (
        lax.psum_scatter(gate_wpart, "gy", scatter_dimension=1, tiled=True),
        lax.psum_scatter(up_wpart, "gy", scatter_dimension=1, tiled=True),
    )
    down_wpart = matmul_tn(hidden_cols, cot_cols)
    grad_down = lax.psum_scatter(down_wpart, "gy", scatter_dimension=1, tiled=True)
    return (layer_out, grad_tokens, grad_gate, grad_up, grad_down)


def solution(mesh):
    placed = (
        P("gy", ("gz", "gx")),
        P("gy", ("gz", "gx")),
        P("gz", ("gx", "gy")),
        P("gz", ("gx", "gy")),
        P("gx", ("gz", "gy")),
    )
    return jax.shard_map(
        local,
        mesh=mesh,
        in_specs=placed,
        out_specs=(
            P("gy", ("gz", "gx")),
            P("gy", ("gz", "gx")),
            P("gz", ("gx", "gy")),
            P("gz", ("gx", "gy")),
            P("gx", ("gz", "gy")),
        ),
        check_vma=False,
    )
```

profile of v0, /device:TPU:0, one launch (start us, length us, event | category | flops | bytes accessed | tf_op | source)
XLA Modules:
  0.0 651.7 jit_solution(4329147587123546220)
XLA Ops:
  7.2 0.0 all-gather.13.cloned.1.call-start
  7.2 0.7 all-gather.13.cloned.1.call-update
  7.9 0.0 all-gather.9.cloned.1.call-start
  7.9 0.7 all-gather.9.cloned.1.call-update
  8.7 0.0 all-gather.7.cloned.1.call-start
  8.7 0.7 all-gather.7.cloned.1.call-update
  9.4 0.0 reduce-scatter.15.cloned.1.call-start
  9.4 26.9 %all_gather.29 = bf16[256,1024]{1,0:T(8,128)(2,1)S(1)} all-gather(bf16[256,128]{1,0:T(8,128)(2,1)} %param.6), channel_id=1, replica_groups=mesh['gx'=8,'gy'=4,'gz'=4] {'gx'}, dimensions={1}, use_global_device_ids=true | all-gather | bytes 589824 | tf_op jit(solution)/shard_map/all_gather | solution.py:40
  36.3 0.0 copy-start.3
  36.3 19.8 %all-gather.13.cloned.1.call-done = bf16[2048,1024]{1,0:T(8,128)(2,1)} async-done(((bf16[2048,256]{1,0:T(8,128)(2,1)}), bf16[2048,1024]{1,0:T(8,128)(2,1)}) %all-gather.13.cloned.1.call-update) | async-done | bytes 4194320 | tf_op jit(solution)/shard_map/all_gather | solution.py:25
  56.2 4.8 fusion.4
  60.9 0.0 reduce-scatter.15.cloned.1.call-update
  61.0 0.0 reduce-scatter.11.cloned.1.call-start
  61.0 0.0 copy-done.3
  61.0 26.5 %all_gather.24 = bf16[256,1024]{1,0:T(8,128)(2,1)S(1)} all-gather(bf16[256,128]{1,0:T(8,128)(2,1)S(1)} %copy-done.3), channel_id=1, replica_groups=mesh['gx'=8,'gy'=4,'gz'=4] {'gx'}, dimensions={1}, use_global_device_ids=true | all-gather | bytes 589824 | tf_op jit(solution)/shard_map/all_gather | solution.py:20
  87.5 14.1 %all-gather.9.cloned.1.call-done = bf16[1024,2048]{1,0:T(8,128)(2,1)} async-done(((bf16[1024,512]{1,0:T(8,128)(2,1)}), bf16[1024,2048]{1,0:T(8,128)(2,1)}) %all-gather.9.cloned.1.call-update) | async-done | bytes 4194320 | tf_op jit(solution)/shard_map/all_gather | solution.py:23
  101.7 4.8 fusion.2
  106.4 0.0 reduce-scatter.11.cloned.1.call-update
  106.5 0.0 reduce-scatter.9.cloned.1.call-start
  106.5 34.9 %all-gather.7.cloned.1.call-done = bf16[1024,2048]{1,0:T(8,128)(2,1)} async-done(((bf16[1024,512]{1,0:T(8,128)(2,1)}), bf16[1024,2048]{1,0:T(8,128)(2,1)}) %all-gather.7.cloned.1.call-update) | async-done | bytes 4194320 | tf_op jit(solution)/shard_map/all_gather | solution.py:22
  141.4 4.8 fusion.1
  146.2 0.0 reduce-scatter.9.cloned.1.call-update
  146.2 0.0 all-gather.15.cloned.1.call-start
  146.2 27.3 %reduce-scatter.15.cloned.1.call-done = f32[256,512]{1,0:T(8,128)} async-done(((f32[256,2048]{1,0:T(8,128)}), f32[256,512]{1,0:T(8,128)}) %reduce-scatter.15.cloned.1.call-update) | async-done | bytes 524304 | tf_op jit(solution)/shard_map/reduce_scatter | solution.py:42
  173.6 32.5 %reduce-scatter.11.cloned.1.call-done = f32[256,512]{1,0:T(8,128)} async-done(((f32[256,2048]{1,0:T(8,128)}), f32[256,512]{1,0:T(8,128)}) %reduce-scatter.11.cloned.1.call-update) | async-done | bytes 524304 | tf_op jit(solution)/shard_map/reduce_scatter | solution.py:30
  206.0 32.4 %reduce-scatter.9.cloned.1.call-done = f32[256,512]{1,0:T(8,128)} async-done(((f32[256,2048]{1,0:T(8,128)}), f32[256,512]{1,0:T(8,128)}) %reduce-scatter.9.cloned.1.call-update) | async-done | bytes 524304 | tf_op jit(solution)/shard_map/reduce_scatter | solution.py:29
  238.4 2.6 multiply_convert_fusion
  241.0 0.0 all-gather.15.cloned.1.call-update
  241.0 0.0 all-gather.17.cloned.1.call-start
  241.1 0.7 all-gather.17.cloned.1.call-update
  241.8 0.0 all-gather.11.cloned.1.call-start
  241.8 0.7 all-gather.11.cloned.1.call-update
  242.5 0.0 reduce-scatter.17.cloned.1.call-start
  242.5 22.4 %all-gather.15.cloned.1.call-done = bf16[256,2048]{1,0:T(8,128)(2,1)} async-done(((bf16[256,512]{1,0:T(8,128)(2,1)}), bf16[256,2048]{1,0:T(8,128)(2,1)}) %all-gather.15.cloned.1.call-update) | async-done | bytes 1048592 | tf_op jit(solution)/shard_map/all_gather | solution.py:46
  264.9 3.8 fusion.5
  268.7 23.2 %all-gather.17.cloned.1.call-done = bf16[256,2048]{1,0:T(8,128)(2,1)} async-done(((bf16[256,512]{1,0:T(8,128)(2,1)}), bf16[256,2048]{1,0:T(8,128)(2,1)}) %all-gather.17.cloned.1.call-update) | async-done | bytes 1048592 | tf_op jit(solution)/shard_map/all_gather | solution.py:47
  291.9 4.8 convolution_add_fusion
  296.6 0.0 reduce-scatter.17.cloned.1.call-update
  296.7 0.0 copy-start.2
  296.7 0.0 reduce-scatter.13.cloned.1.call-start
  296.7 21.5 %all-gather.11.cloned.1.call-done = bf16[256,2048]{1,0:T(8,128)(2,1)} async-done(((bf16[256,512]{1,0:T(8,128)(2,1)}), bf16[256,2048]{1,0:T(8,128)(2,1)}) %all-gather.11.cloned.1.call-update) | async-done | bytes 1048592 | tf_op jit(solution)/shard_map/all_gather | solution.py:35
  318.3 4.7 fusion.3
  323.0 0.0 reduce-scatter.13.cloned.1.call-update
  323.0 0.0 reduce-scatter.21.cloned.1.call-start
  323.1 0.0 copy-done.2
  323.1 4.5 convolution_bitcast_fusion
  327.6 0.0 reduce-scatter.21.cloned.1.call-update
  327.6 0.0 reduce-scatter.19.cloned.1.call-start
  327.7 1.1 copy-done
  328.8 4.5 convolution_bitcast_fusion.1
  333.4 0.0 reduce-scatter.19.cloned.1.call-update
  333.4 0.0 reduce-scatter.23.cloned.1.call-start
  333.4 1.1 copy-done.1
  334.6 4.5 fusion.6
  339.1 0.0 reduce-scatter.23.cloned.1.call-update
  339.1 22.0 %reduce-scatter.17.cloned.1.call-done = f32[256,128]{1,0:T(8,128)} async-done(((f32[256,1024]{1,0:T(8,128)}), f32[256,128]{1,0:T(8,128)}) %reduce-scatter.17.cloned.1.call-update) | async-done | bytes 131088 | tf_op jit(solution)/shard_map/reduce_scatter | solution.py:50
  361.1 1.5 convert_element_type.19
  362.7 40.0 %reduce-scatter.13.cloned.1.call-done = f32[256,128]{1,0:T(8,128)} async-done(((f32[256,1024]{1,0:T(8,128)}), f32[256,128]{1,0:T(8,128)}) %reduce-scatter.13.cloned.1.call-update) | async-done | bytes 131088 | tf_op jit(solution)/shard_map/reduce_scatter | solution.py:37
  402.7 1.5 convert_element_type.16
  404.2 78.8 %reduce-scatter.21.cloned.1.call-done = f32[1024,512]{0,1:T(8,128)} async-done(((f32[1024,2048]{0,1:T(8,128)}), f32[1024,512]{0,1:T(8,128)}) %reduce-scatter.21.cloned.1.call-update) | async-done | bytes 2097168 | tf_op jit(solution)/shard_map/reduce_scatter | solution.py:57
  483.0 2.9 copy.11
  485.9 77.9 %reduce-scatter.19.cloned.1.call-done = f32[1024,512]{0,1:T(8,128)} async-done(((f32[1024,2048]{0,1:T(8,128)}), f32[1024,512]{0,1:T(8,128)}) %reduce-scatter.19.cloned.1.call-update) | async-done | bytes 2097168 | tf_op jit(solution)/shard_map/reduce_scatter | solution.py:56
  563.8 2.9 copy.10
  566.7 78.5 %reduce-scatter.23.cloned.1.call-done = f32[2048,256]{1,0:T(8,128)} async-done(((f32[2048,1024]{1,0:T(8,128)}), f32[2048,256]{1,0:T(8,128)}) %reduce-scatter.23.cloned.1.call-update) | async-done | bytes 2097168 | tf_op jit(solution)/shard_map/reduce_scatter | solution.py:60
  (2 shorter events, 0.0 us)
Async XLA Ops:
  7.2 49.0 %all-gather.13.cloned.1.call-start = ((), (), s32[]{:S(2)}) async-start(), calls=%async_computation.13 | async-start | bytes 5242880 | tf_op jit(solution)/shard_map/all_gather | solution.py:25
  7.9 93.8 %all-gather.9.cloned.1.call-start = ((), (), s32[]{:S(2)}) async-start(), calls=%async_computation.10 | async-start | bytes 5242880 | tf_op jit(solution)/shard_map/all_gather | solution.py:23
  8.7 132.8 %all-gather.7.cloned.1.call-start = ((), (), s32[]{:S(2)}) async-start(), calls=%async_computation.8 | async-start | bytes 5242880 | tf_op jit(solution)/shard_map/all_gather | solution.py:22
  9.4 164.2 %reduce-scatter.15.cloned.1.call-start = ((), (), s32[]{:S(2)}) async-start(), calls=%async_computation.15 | async-start | bytes 2621440 | tf_op jit(solution)/shard_map/reduce_scatter | solution.py:42
  36.3 24.7 %copy-start.3 = (bf16[256,128]{1,0:T(8,128)(2,1)S(1)}, bf16[256,128]{1,0:T(8,128)(2,1)}, u32[]{:S(2)}) copy-start(bf16[256,128]{1,0:T(8,128)(2,1)} %param.5) | copy-start | bytes 196612
  61.0 145.1 %reduce-scatter.11.cloned.1.call-start = ((), (), s32[]{:S(2)}) async-start(), calls=%async_computation.11 | async-start | bytes 2621440 | tf_op jit(solution)/shard_map/reduce_scatter | solution.py:30
  106.5 131.9 %reduce-scatter.9.cloned.1.call-start = ((), (), s32[]{:S(2)}) async-start(), calls=%async_computation.9 | async-start | bytes 2621440 | tf_op jit(solution)/shard_map/reduce_scatter | solution.py:29
  146.2 118.7 %all-gather.15.cloned.1.call-start = ((), (), s32[]{:S(2)}) async-start(), calls=%async_computation.16 | async-start | bytes 1310720 | tf_op jit(solution)/shard_map/all_gather | solution.py:46
  241.0 50.9 %all-gather.17.cloned.1.call-start = ((), (), s32[]{:S(2)}) async-start(), calls=%async_computation.17 | async-start | bytes 1310720 | tf_op jit(solution)/shard_map/all_gather | solution.py:47
  241.8 76.5 %all-gather.11.cloned.1.call-start = ((), (), s32[]{:S(2)}) async-start(), calls=%async_computation.12 | async-start | bytes 1310720 | tf_op jit(solution)/shard_map/all_gather | solution.py:35
  242.5 118.6 %reduce-scatter.17.cloned.1.call-start = ((), (), s32[]{:S(2)}) async-start(), calls=%async_computation.18 | async-start | bytes 1179648 | tf_op jit(solution)/shard_map/reduce_scatter | solution.py:50
  296.7 26.4 %copy-start.2 = (bf16[256,2048]{1,0:T(8,128)(2,1)S(1)}, bf16[256,2048]{1,0:T(8,128)(2,1)}, u32[]{:S(2)}) copy-start(bf16[256,2048]{1,0:T(8,128)(2,1)} %all-gather.17.cloned.1.call-done) | copy-start | bytes 3145732
  296.7 106.0 %reduce-scatter.13.cloned.1.call-start = ((), (), s32[]{:S(2)}) async-start(), calls=%async_computation.14 | async-start | bytes 1179648 | tf_op jit(solution)/shard_map/reduce_scatter | solution.py:37
  323.0 160.0 %reduce-scatter.21.cloned.1.call-start = ((), (), s32[]{:S(2)}) async-start(), calls=%async_computation.20 | async-start | bytes 10485760 | tf_op jit(solution)/shard_map/reduce_scatter | solution.py:57
  327.6 1.2 copy-start
  327.6 236.1 %reduce-scatter.19.cloned.1.call-start = ((), (), s32[]{:S(2)}) async-start(), calls=%async_computation.19 | async-start | bytes 10485760 | tf_op jit(solution)/shard_map/reduce_scatter | solution.py:56
  333.4 1.2 copy-start.1
  333.4 311.8 %reduce-scatter.23.cloned.1.call-start = ((), (), s32[]{:S(2)}) async-start(), calls=%async_computation.21 | async-start | bytes 10485760 | tf_op jit(solution)/shard_map/reduce_scatter | solution.py:60
Sparse Core Ops, SparseCore 0:
  9.7 46.4 all-gather.12
  57.8 43.8 all-gather.8
  103.4 38.0 all-gather.6
  144.2 29.2 reduce-scatter.14
  176.5 29.4 reduce-scatter.10
  208.9 29.4 reduce-scatter.8
  241.1 23.7 all-gather.14
  267.2 24.5 all-gather.16
  293.6 24.5 all-gather.10
  321.2 39.9 reduce-scatter.16
  364.2 38.4 reduce-scatter.12
  405.4 77.5 reduce-scatter.20
  485.7 78.0 reduce-scatter.18
  567.1 78.0 reduce-scatter.22
where the time goes:
time: 653 us; the launch traced here: 652 us
  waiting for transfers between devices  529 us (81%)
  blocking collectives  53.4 us (8%)
  matrix products  41.2 us (6%)
  between operations  14 us (2%)
  local copies, waits for them, and re-layouts  8.07 us (1%)
    reduce_scatter x1, waiting for transfers between devices, local(): lax.psum_scatter(up_wpart, 'gy', scatter_dimension=1, tiled=True)  78.8 us
    reduce_scatter x1, waiting for transfers between devices, local(): lax.psum_scatter(down_wpart, 'gy', scatter_dimension=1, tiled=True)  78.5 us
    reduce_scatter x1, waiting for transfers between devices, local(): lax.psum_scatter(gate_wpart, 'gy', scatter_dimension=1, tiled=True)  77.9 us
    reduce_scatter x1, waiting for transfers between devices, local(): lax.psum_scatter(out_part, 'gx', scatter_dimension=1, tiled=True)  40 us
    all_gather x1, waiting for transfers between devices, local(): lax.all_gather(gate_weight, 'gy', axis=1, tiled=True)  34.9 us
    reduce_scatter x1, waiting for transfers between devices, local(): lax.psum_scatter(up_part, 'gz', scatter_dimension=1, tiled=True)  32.5 us
    reduce_scatter x1, waiting for transfers between devices, local(): lax.psum_scatter(gate_part, 'gz', scatter_dimension=1, tiled=True)  32.4 us
    reduce_scatter x1, waiting for transfers between devices, local(): lax.psum_scatter(hidden_grad_part, 'gz', scatter_dimension=1, tiled=True)  27.3 us
  transfers between devices with their start and end apart: 14, of which 14 were waited for; matrix products, arithmetic and copies ran while one was open for 8% of the time, Pallas kernels for 0%

commit v1 on v0

v1 whole, which is shorter than its diff:
```python
import jax
import jax.numpy as jnp
from jax import lax
from jax.experimental import pallas as pl
from jax.experimental.pallas import tpu as pltpu
from jax.sharding import PartitionSpec as P

MESH = pl.DeviceIdType.MESH
BF, F32 = jnp.bfloat16, jnp.float32
XT = jnp.bfloat16
YT = jnp.float32
NSEM = 160


def dot(a, b, dims):
    return lax.dot_general(a, b, (dims, ((), ())), preferred_element_type=F32)


class Net:
    def __init__(self, send, recv):
        self.send, self.recv, self.used, self.out = send, recv, 0, []

    def slot(self):
        self.used += 1
        return self.used - 1

    def push(self, src, dst, device, k=None):
        k = self.slot() if k is None else k
        copy = pltpu.make_async_remote_copy(
            src_ref=src, dst_ref=dst, send_sem=self.send.at[k], recv_sem=self.recv.at[k],
            device_id=device, device_id_type=MESH)
        copy.start()
        self.out.append(copy)
        return k

    def local(self, src, dst):
        k = self.slot()
        copy = pltpu.make_async_copy(src, dst, self.recv.at[k])
        copy.start()
        return copy

    def arrived(self, k, landing):
        pltpu.make_async_copy(landing, landing, self.recv.at[k]).wait()

    def drain(self):
        for copy in self.out:
            copy.wait_send()
        self.out = []


class ReduceScatter:
    def __init__(self, net, part, sent, half, full, pos, plus, minus):
        self.net, self.part, self.sent, self.half, self.full = net, part, sent, half, full
        self.pos, self.plus, self.minus = pos, plus, minus
        self.rows = sent.shape[1]

    def start(self):
        m = self.rows // 2
        sent, net = self.sent, self.net
        sent[0] = self.part[(self.pos + 2) % 4].astype(sent.dtype)
        self.ka = net.push(sent.at[0, pl.ds(0, m)], self.half.at[0], self.plus)
        self.kb = net.push(sent.at[0, pl.ds(m, m)], self.half.at[1], self.minus)

    def middle(self):
        m = self.rows // 2
        sent, net, half = self.sent, self.net, self.half
        right, left = (self.pos + 1) % 4, (self.pos + 3) % 4
        sent[1, m:] = self.part[right, m:].astype(sent.dtype)
        sent[2, :m] = self.part[left, :m].astype(sent.dtype)
        net.arrived(self.ka, half.at[0])
        sent[1, :m] = (self.part[right, :m] + half[0].astype(F32)).astype(sent.dtype)
        self.kp = net.push(sent.at[1], self.full.at[0], self.plus)
        net.arrived(self.kb, half.at[1])
        sent[2, m:] = (self.part[left, m:] + half[1].astype(F32)).astype(sent.dtype)
        self.km = net.push(sent.at[2], self.full.at[1], self.minus)

    def finish(self):
        self.net.arrived(self.kp, self.full.at[0])
        self.net.arrived(self.km, self.full.at[1])
        return self.part[self.pos] + self.full[0].astype(F32) + self.full[1].astype(F32)


class AllGather:
    def __init__(self, net, slots, pos, plus, minus):
        self.net, self.slots, self.pos, self.plus, self.minus = net, slots, pos, plus, minus
        self.rows = slots.shape[1]

    def start(self):
        own = self.slots.at[self.pos]
        self.kp = self.net.push(own, own, self.plus)
        self.km = self.net.push(own, own, self.minus)

    def forward(self):
        m = self.rows // 2
        right, left = (self.pos + 1) % 4, (self.pos + 3) % 4
        self.net.arrived(self.kp, self.slots.at[left])
        first = self.slots.at[left, pl.ds(0, m)]
        self.ka = self.net.push(first, first, self.plus)
        self.net.arrived(self.km, self.slots.at[right])
        second = self.slots.at[right, pl.ds(m, m)]
        self.kb = self.net.push(second, second, self.minus)

    def finish(self):
        m = self.rows // 2
        far = (self.pos + 2) % 4
        self.net.arrived(self.ka, self.slots.at[far, pl.ds(0, m)])
        self.net.arrived(self.kb, self.slots.at[far, pl.ds(m, m)])


def kernel(tok, cot, wg, wu, wd, lo, gt, t_out, g_out, gd_out,
           T, C, W, V, H, G, PG, PH, GU, sg, hg, fg, sh, hh, fh,
           own, give, take, sx, hx, fx, sy, ry, gs, gr, send, recv):
    gx, gy, gz = lax.axis_index("gx"), lax.axis_index("gy"), lax.axis_index("gz")
    x, z, c = gx // 2, gz, gy % 2
    yh, yl = gy // 2, gx % 2
    y = yh * 2 + yl

    def at(x, y, z, c):
        return (x * 2 + y % 2, (y // 2) * 2 + c, z)

    ys = [at(x, (y + d) % 4, z, c) for d in (1, 2, 3)]
    xs = [at((x + d) % 4, y, z, c) for d in (1, 2, 3)]
    zp, zm = at(x, y, (z + 1) % 4, c), at(x, y, (z + 3) % 4, c)
    mate = at(x, y, z, 1 - c)
    cross = at(x, (y + 2) % 4, z, 1 - c)
    net = Net(send, recv)

    loads = [net.local(tok, T.at[gy, :, pl.ds(pl.multiple_of(gx * 128, 128), 128)]),
             net.local(cot, C.at[gy, :, pl.ds(pl.multiple_of(gx * 128, 128), 128)])]
    w_loads = [net.local(wg, W.at[:, pl.ds(0, 512)]), net.local(wu, W.at[:, pl.ds(512, 512)])]
    v_load = net.local(wd.at[pl.ds(pl.multiple_of(gy * 512, 512), 512)],
                       V.at[:, pl.ds(pl.multiple_of(gy * 256, 256), 256)])

    barrier = pltpu.get_barrier_semaphore()
    peers = ys + xs + [zp, zm, mate, cross]
    for peer in peers:
        pl.semaphore_signal(barrier, inc=1, device_id=peer, device_id_type=MESH)
    pl.semaphore_wait(barrier, len(peers))

    def gather_y(src, buf):
        mine = buf.at[gy, :, pl.ds(pl.multiple_of(gx * 128, 128), 128)]
        ks = [net.push(src, mine, d) for d in ys]

        def done():
            for d, k in zip((3, 2, 1), ks):
                yy = (y + d) % 4
                g2, col = (yy // 2) * 2 + c, pl.multiple_of((x * 2 + yy % 2) * 128, 128)
                net.arrived(k, buf.at[g2, :, pl.ds(col, 128)])
        return done

    def gather_x(buf, h):
        g2 = h * 2 + c
        mine = buf.at[g2, :, pl.ds(pl.multiple_of(x * 256, 256), 256)]
        ks = [net.push(mine, mine, d) for d in xs]

        def done():
            for d, k in zip((3, 2, 1), ks):
                net.arrived(k, buf.at[g2, :, pl.ds(pl.multiple_of(((x + d) % 4) * 256, 256), 256)])
        return done

    def share(buf, h):
        mine = buf.at[h * 2 + c]
        k = net.push(mine, mine, mate)
        return lambda: net.arrived(k, buf.at[h * 2 + 1 - c])

    chunk = [c, 1 - c, 2 + 1 - c, 2 + c]

    rs_g = [ReduceScatter(net, PG.at[i], sg.at[i], hg.at[i], fg.at[i], z, zp, zm) for i in range(4)]
    rs_h = [ReduceScatter(net, PH.at[i], sh.at[i], hh.at[i], fh.at[i], z, zp, zm) for i in range(4)]
    ag_h = [AllGather(net, H.at[chunk[i]], z, zp, zm) for i in range(4)]
    ag_g = [AllGather(net, G.at[chunk[i]], z, zp, zm) for i in range(4)]

    def g1(i):
        def body(n, _):
            cols = pl.ds(pl.multiple_of(n * 256, 256), 256)
            PG[i, :, :, cols] = dot(T[chunk[i]], W[:, cols], ((1,), (0,))).reshape(4, 64, 256)
            return 0
        lax.fori_loop(0, 4, body, 0)
        rs_g[i].start()

    def g3(i):
        s = rs_g[i].finish()
        GU[i] = s
        gate, up = s[:, :512], s[:, 512:]
        H[chunk[i], z] = (gate * jax.nn.sigmoid(gate) * up).astype(BF)
        ag_h[i].start()

    def h1(i):
        def body(n, _):
            rows = pl.ds(pl.multiple_of(n * 256, 256), 256)
            PH[i, :, :, rows] = dot(C[chunk[i]], V[rows, :], ((1,), (1,))).reshape(4, 64, 256)
            return 0
        lax.fori_loop(0, 2, body, 0)
        rs_h[i].start()

    def h3(i):
        grad = rs_h[i].finish()
        gate, up = GU[i, :, :512], GU[i, :, 512:]
        s = jax.nn.sigmoid(gate)
        G[chunk[i], z, :, :512] = (grad * up * s * (1.0 + gate * (1.0 - s))).astype(BF)
        G[chunk[i], z, :, 512:] = (grad * (gate * s)).astype(BF)
        ag_g[i].start()

    took = {}

    def place(m, i):
        return (own.at[m, 0], give.at[m, 0], give.at[m, 1], own.at[m, 1])[i]

    def give_mate(m, i):
        if i in (1, 2):
            took[m, i - 1] = net.push(give.at[m, i - 1], take.at[m, i - 1], mate)

    def g5(i):
        ag_h[i].finish()
        dst = place(0, i)

        def body(n, _):
            cols = pl.ds(pl.multiple_of(n * 256, 256), 256)
            dst[n] = dot(H[chunk[i]].reshape(256, 512), V[:, cols], ((1,), (0,)))
            return 0
        lax.fori_loop(0, 4, body, 0)
        give_mate(0, i)

    def h5(i):
        ag_g[i].finish()
        dst = place(1, i)

        def body(n, _):
            rows = pl.ds(pl.multiple_of(n * 256, 256), 256)
            dst[n] = dot(G[chunk[i]].reshape(256, 1024), W[rows, :], ((1,), (1,)))
            return 0
        lax.fori_loop(0, 4, body, 0)
        give_mate(1, i)

    rs_x = [[ReduceScatter(net, own.at[m, o], sx.at[m, o], hx.at[m, o], fx.at[m, o], x, xs[0], xs[2])
             for o in range(2)] for m in range(2)]

    def x1(m, o):
        net.arrived(took[m, o], take.at[m, o])

        def body(n, _):
            own[m, o, n] += take[m, o, n]
            return 0
        lax.fori_loop(0, 4, body, 0)
        rs_x[m][o].start()

    ky = [[[net.slot() for _ in range(3)] for _ in range(2)] for _ in range(2)]

    def y_copy(m, o, t, d):
        k = ky[m][o][d - 1]
        return pltpu.make_async_remote_copy(
            src_ref=sy.at[m, o, t], dst_ref=ry.at[m, d - 1],
            send_sem=send.at[k], recv_sem=recv.at[k],
            device_id=at(x, 2 * o + t, z, c), device_id_type=MESH)

    def x3(m, o):
        r = rs_x[m][o].finish()
        sy[m, o, 0] = r[:, :128].astype(YT)
        sy[m, o, 1] = r[:, 128:].astype(YT)
        for t in range(2):
            for d in (1, 2, 3):
                @pl.when((y + d) % 4 == 2 * o + t)
                def _():
                    y_copy(m, o, t, d).start()

    def y_sent(m, o):
        for t in range(2):
            for d in (1, 2, 3):
                @pl.when((y + d) % 4 == 2 * o + t)
                def _():
                    y_copy(m, o, t, d).wait_send()

    def y_done(m, o, out):
        @pl.when(yh == o)
        def _():
            total = sy[m, o, yl].astype(F32)
            for d in (1, 2, 3):
                net.arrived(ky[m][o][d - 1], ry.at[m, d - 1])
                total += ry[m, d - 1].astype(F32)
            out[...] = total.astype(BF)

    gk = []

    def down_grad():
        def body(g, _):
            cols = pl.ds(pl.multiple_of(g * 256, 256), 256)
            gs[g] = dot(H[...].reshape(1024, 512), C[:, :, cols].reshape(1024, 256), ((0,), (0,))).astype(BF)
            return 0
        lax.fori_loop(0, 4, body, 0)
        g_mate, g_y, g_cross = yh * 2 + 1 - c, (1 - yh) * 2 + c, (1 - yh) * 2 + 1 - c
        gk.append((net.push(gs.at[g_y], gr.at[gy], ys[1]), g_y))
        gk.append((net.push(gs.at[g_cross], gr.at[gy], cross), g_cross))
        gk.append((net.push(gs.at[g_mate], gr.at[gy], mate), g_mate))
        gr[gy] = gs[gy]

    def down_share():
        g_mate, g_y, g_cross = yh * 2 + 1 - c, (1 - yh) * 2 + c, (1 - yh) * 2 + 1 - c
        dst = V.at[:, pl.ds(pl.multiple_of(gy * 256, 256), 256)]

        def rows(g):
            return wd.at[pl.ds(pl.multiple_of(g * 512, 512), 512)]
        ks = [(net.push(rows(g_y), dst, ys[1]), g_y), (net.push(rows(g_cross), dst, cross), g_cross),
              (net.push(rows(g_mate), dst, mate), g_mate)]

        def done():
            for k, g in ks:
                net.arrived(k, V.at[:, pl.ds(pl.multiple_of(g * 256, 256), 256)])
            v_load.wait()
        return done

    ty = gather_y(tok, T)
    for copy in loads:
        copy.wait()
    ty()
    tx = [gather_x(T, 0), gather_x(T, 1)]
    cy = gather_y(cot, C)
    vs = down_share()
    for copy in w_loads:
        copy.wait()
    tx[0]()
    t_mate = [share(T, 0)]
    g1(0)
    t_mate[0]()
    g1(1)
    rs_g[0].middle()
    tx[1]()
    t_mate.append(share(T, 1))
    cy()
    cx = [gather_x(C, 0), gather_x(C, 1)]
    t_mate[1]()
    g1(2)
    rs_g[1].middle()
    g3(0)
    g1(3)
    keep = [net.local(T, t_out)]
    rs_g[2].middle()
    g3(1)
    ag_h[0].forward()
    rs_g[3].middle()
    g3(2)
    ag_h[1].forward()
    vs()
    cx[0]()
    c_mate = [share(C, 0)]
    h1(0)
    g5(0)
    g3(3)
    ag_h[2].forward()
    c_mate[0]()
    h1(1)
    g5(1)
    rs_h[0].middle()
    ag_h[3].forward()
    cx[1]()
    c_mate.append(share(C, 1))
    x1(0, 0)
    g5(2)
    c_mate[1]()
    h1(2)
    rs_h[1].middle()
    h3(0)
    rs_x[0][0].middle()
    g5(3)
    x1(0, 1)
    h1(3)
    rs_h[2].middle()
    h3(1)
    ag_g[0].forward()
    x3(0, 0)
    down_grad()
    rs_x[0][1].middle()
    rs_h[3].middle()
    h3(2)
    ag_g[1].forward()
    h5(0)
    h3(3)
    ag_g[2].forward()
    h5(1)
    x3(0, 1)
    x1(1, 0)
    ag_g[3].forward()
    h5(2)
    rs_x[1][0].middle()
    h5(3)
    keep.append(net.local(G, g_out))
    x1(1, 1)
    rs_x[1][1].middle()
    x3(1, 0)
    for k, g in gk:
        net.arrived(k, gr.at[g])
    keep.append(net.local(gr, gd_out))
    y_done(0, 0, lo)
    y_done(0, 1, lo)
    x3(1, 1)
    y_done(1, 0, gt)
    y_done(1, 1, gt)
    for copy in keep:
        copy.wait()
    for m in range(2):
        for o in range(2):
            y_sent(m, o)
    net.drain()


def local(tok, cot, wg, wu, wd):
    any_, vmem = pl.BlockSpec(memory_space=pl.ANY), pl.BlockSpec(memory_space=pltpu.VMEM)
    S = jax.ShapeDtypeStruct
    scratch = [
        pltpu.VMEM((4, 256, 1024), BF),
        pltpu.VMEM((4, 256, 1024), BF),
        pltpu.VMEM((1024, 1024), BF),
        pltpu.VMEM((512, 1024), BF),
        pltpu.VMEM((4, 4, 64, 512), BF),
        pltpu.VMEM((4, 4, 64, 1024), BF),
        pltpu.VMEM((4, 4, 64, 1024), F32),
        pltpu.VMEM((4, 4, 64, 512), F32),
        pltpu.VMEM((4, 64, 1024), F32),
        pltpu.VMEM((4, 3, 64, 1024), BF),
        pltpu.VMEM((4, 2, 32, 1024), BF),
        pltpu.VMEM((4, 2, 64, 1024), BF),
        pltpu.VMEM((4, 3, 64, 512), BF),
        pltpu.VMEM((4, 2, 32, 512), BF),
        pltpu.VMEM((4, 2, 64, 512), BF),
        pltpu.VMEM((2, 2, 4, 256, 256), F32),
        pltpu.VMEM((2, 2, 4, 256, 256), F32),
        pltpu.VMEM((2, 2, 4, 256, 256), F32),
        pltpu.VMEM((2, 2, 3, 256, 256), XT),
        pltpu.VMEM((2, 2, 2, 128, 256), XT),
        pltpu.VMEM((2, 2, 2, 256, 256), XT),
        pltpu.VMEM((2, 2, 2, 256, 128), YT),
        pltpu.VMEM((2, 3, 256, 128), YT),
        pltpu.VMEM((4, 512, 256), BF),
        pltpu.VMEM((4, 512, 256), BF),
        pltpu.SemaphoreType.DMA((NSEM,)),
        pltpu.SemaphoreType.DMA((NSEM,)),
    ]
    lo, gt, t_all, g_all, gd = pl.pallas_call(
        kernel,
        out_shape=[S((256, 128), BF), S((256, 128), BF), S((4, 256, 1024), BF),
                   S((4, 4, 64, 1024), BF), S((4, 512, 256), BF)],
        in_specs=[any_] * 5,
        out_specs=[vmem, vmem, any_, any_, any_],
        scratch_shapes=scratch,
        compiler_params=pltpu.CompilerParams(
            collective_id=0, has_side_effects=True, vmem_limit_bytes=56 << 20),
        cost_estimate=pl.CostEstimate(flops=8_000_000_000, bytes_accessed=10_000_000, transcendentals=600_000),
        name="layer",
    )(tok, cot, wg, wu, wd)
    t_all = t_all.reshape(1024, 1024)
    g_all = g_all.reshape(1024, 1024)
    tn = ((0,), (0,))
    grad_gate = dot(t_all, g_all[:, :512], tn)
    grad_up = dot(t_all, g_all[:, 512:], tn)
    return lo, gt, grad_gate, grad_up, gd.reshape(2048, 256).astype(F32)


def solution(mesh):
    ins = (P("gy", ("gz", "gx")), P("gy", ("gz", "gx")), P("gz", ("gx", "gy")),
           P("gz", ("gx", "gy")), P("gx", ("gz", "gy")))
    outs = (P("gy", ("gz", "gx")), P("gy", ("gz", "gx")), P("gz", ("gx", "gy")),
            P("gz", ("gx", "gy")), P("gx", ("gz", "gy")))
    return jax.shard_map(local, mesh=mesh, in_specs=ins, out_specs=outs, check_vma=False)
```

time: 653 us -> 111 us (0.17)
  waiting for transfers between devices: 529 us -> 0 us
  Pallas kernels: 0 us -> 99 us
  blocking collectives: 53.4 us -> 0 us
  matrix products: 41.2 us -> 7.22 us
  between operations: 14 us -> 0.67 us
  local copies, waits for them, and re-layouts: 8.07 us -> 1.28 us
    reduce_scatter x8 -> x0, waiting for transfers between devices: 389 us -> none  [the longest x1 78.8 us: local(): lax.psum_scatter(up_wpart, 'gy', scatter_dimension=1, tiled=True)]
    all_gather x6 -> x0, waiting for transfers between devices: 136 us -> none  [the longest x1 34.9 us: local(): lax.all_gather(gate_weight, 'gy', axis=1, tiled=True)]
    pallas_call x0 -> x1, Pallas kernels: none -> 99 us  [local(): pl.pallas_call(kernel, out_shape=[S((256, 128), BF), S((256, 128), BF), S...]
    all_gather x2 -> x0, blocking collectives: 53.4 us -> none  [the longest x1 26.9 us: local(): cot_cols = lax.all_gather(cotangent, 'gx', axis=1, tiled=True)]
    dot_general x9 -> x2, matrix products: 41.2 us -> 7.22 us  [dot(): return lax.dot_general(a, b, (dims, ((), ())), preferred_element_type=F32)]
    unnamed x10 -> x12, local copies, waits for them, and re-layouts: 8.07 us -> 1.28 us
  transfers between devices with their start and end apart: 14 -> 0, of which waited for: 14 -> 0; matrix products, arithmetic and copies ran while one was open for 8% -> 0% of each run, Pallas kernels for 0% -> 0%
where the time goes in v1:
time: 111 us; the launch traced here: 110 us
  Pallas kernels  99 us (89%)
  matrix products  7.22 us (7%)
  other arithmetic  1.55 us (1%)
  local copies, waits for them, and re-layouts  1.28 us (1%)
    pallas_call x1, Pallas kernels, local(): pl.pallas_call(kernel, out_shape=[S((256, 128), BF), S((256, 128), BF), S...  99 us
    dot_general x2, matrix products, dot(): return lax.dot_general(a, b, (dims, ((), ())), preferred_element_type=F32)  7.22 us

profile of v1, /device:TPU:0, one launch (start us, length us, event | category | flops | bytes accessed | tf_op | source)
XLA Modules:
  0.0 109.7 jit_solution(5808954398972414385)
XLA Ops:
  0.6 99.0 %layer.1 = (bf16[256,128]{1,0:T(8,128)(2,1)}, bf16[256,128]{1,0:T(8,128)(2,1)}, bf16[4,256,1024]{2,1,0:T(8,128)(2,1)}, bf16[4,4,64,1024]{3,2,1,0:T(8,128)(2,1)}, bf16[4,512,256]{2,1,0:T(8,128)(2,1)}) custom-call(bf16[256,128]{1,0:T(8,128)(2,1)} %tok.1, bf16[256,128]{1,0:T(8,128)(2,1)} %cot.1, bf16[1024,512]{1,0:T(8,128)(2,1)} %wg.1, bf16[1024,512]{1,0:T(8,128)(2,1)} %wu.1, ...), custom_call_target="tpu_custom_call" | custom-call | flops 8000000000 | bytes 10000000 | tf_op jit(solution)/shard_map/layer/pallas_call | solution.py:437
  99.6 0.0 copy-start.3
  99.6 0.0 copy-start.4
  99.6 4.6 %fusion = f32[1024,512]{1,0:T(8,128)} fusion(bf16[1024,1024]{1,0:T(8,128)(2,1)} %bitcast.7, bf16[1024,1024]{1,0:T(8,128)(2,1)} %bitcast.9), kind=kOutput, calls=%fused_computation | convolution fusion | flops 1073741824 | bytes 5242880 | tf_op jit(solution)/shard_map/dot_general | solution.py:16
  104.2 0.0 copy-done.3
  104.2 0.0 copy-done.4
  104.2 0.0 copy-start
  104.2 2.6 %fusion.2 = f32[1024,512]{1,0:T(8,128)} fusion(bf16[1024,1024]{1,0:T(8,128)(2,1)S(1)} %bitcast.8, bf16[1024,1024]{1,0:T(8,128)(2,1)S(1)} %bitcast.10), kind=kOutput, calls=%fused_computation.2 | convolution fusion | flops 1073741824 | bytes 5242880 | tf_op jit(solution)/shard_map/dot_general | solution.py:16
  106.9 0.0 copy-done
  106.9 0.0 copy-start.2
  106.9 0.0 copy-start.1
  106.9 1.5 %bitcast_convert_fusion = f32[2048,256]{1,0:T(8,128)} fusion(bf16[4,512,256]{2,1,0:T(8,128)(2,1)S(1)} %copy-done), kind=kLoop, calls=%fused_computation.4 | loop fusion | flops 524288 | bytes 3145728 | tf_op jit(solution)/shard_map/convert_element_type | solution.py:454
  108.4 0.0 copy-done.2
  108.4 0.6 copy.12
  109.0 0.0 copy-done.1
  109.0 0.6 copy.13
Async XLA Ops:
  99.6 4.6 %copy-start.3 = (bf16[4,256,1024]{2,1,0:T(8,128)(2,1)S(1)}, bf16[4,256,1024]{2,1,0:T(8,128)(2,1)}, u32[]{:S(2)}) copy-start(bf16[4,256,1024]{2,1,0:T(8,128)(2,1)} %get-tuple-element.12) | copy-start | bytes 6291460
  99.6 4.6 %copy-start.4 = (bf16[4,4,64,1024]{3,2,1,0:T(8,128)(2,1)S(1)}, bf16[4,4,64,1024]{3,2,1,0:T(8,128)(2,1)}, u32[]{:S(2)}) copy-start(bf16[4,4,64,1024]{3,2,1,0:T(8,128)(2,1)} %get-tuple-element.13) | copy-start | bytes 6291460
  104.2 2.6 %copy-start = (bf16[4,512,256]{2,1,0:T(8,128)(2,1)S(1)}, bf16[4,512,256]{2,1,0:T(8,128)(2,1)}, u32[]{:S(2)}) copy-start(bf16[4,512,256]{2,1,0:T(8,128)(2,1)} %get-tuple-element.14) | copy-start | bytes 3145732
  106.9 1.6 %copy-start.2 = (bf16[256,128]{1,0:T(8,128)(2,1)S(1)}, bf16[256,128]{1,0:T(8,128)(2,1)}, u32[]{:S(2)}) copy-start(bf16[256,128]{1,0:T(8,128)(2,1)} %get-tuple-element.20) | copy-start | bytes 196612
  106.9 2.2 %copy-start.1 = (bf16[256,128]{1,0:T(8,128)(2,1)S(1)}, bf16[256,128]{1,0:T(8,128)(2,1)}, u32[]{:S(2)}) copy-start(bf16[256,128]{1,0:T(8,128)(2,1)} %get-tuple-element.21) | copy-start | bytes 196612

commit v2 on v0

v2 whole, which is shorter than its diff:
```python
import jax
import jax.numpy as jnp
from jax import lax
from jax.experimental import pallas as pl
from jax.experimental.pallas import tpu as pltpu
from jax.sharding import PartitionSpec as P

MESH = pl.DeviceIdType.MESH
BF, F32 = jnp.bfloat16, jnp.float32
XT = jnp.bfloat16
YT = jnp.float32
NSEM = 256
PARTS = (2, 1, 1, 2)
TPARTS = 2


def dot(a, b, dims):
    return lax.dot_general(a, b, (dims, ((), ())), preferred_element_type=F32)


class Net:
    def __init__(self, send, recv):
        self.send, self.recv, self.used, self.out = send, recv, 0, []

    def slot(self):
        self.used += 1
        return self.used - 1

    def push(self, src, dst, device, k=None):
        k = self.slot() if k is None else k
        copy = pltpu.make_async_remote_copy(
            src_ref=src, dst_ref=dst, send_sem=self.send.at[k], recv_sem=self.recv.at[k],
            device_id=device, device_id_type=MESH)
        copy.start()
        self.out.append(copy)
        return k

    def local(self, src, dst):
        k = self.slot()
        copy = pltpu.make_async_copy(src, dst, self.recv.at[k])
        copy.start()
        return copy

    def arrived(self, k, landing):
        pltpu.make_async_copy(landing, landing, self.recv.at[k]).wait()

    def drain(self):
        for copy in self.out:
            copy.wait_send()
        self.out = []


class ReduceScatter:
    def __init__(self, net, part, sent, half, full, rows, pos, plus, minus):
        self.net, self.part, self.sent, self.half, self.full = net, part, sent, half, full
        self.rows, self.pos, self.plus, self.minus = rows, pos, plus, minus

    def start(self):
        m = self.rows // 2
        far = self.sent(0, 0, self.rows)
        far[...] = self.part((self.pos + 2) % 4, 0, self.rows)[...].astype(far.dtype)
        self.ka = self.net.push(self.sent(0, 0, m), self.half(0), self.plus)
        self.kb = self.net.push(self.sent(0, m, m), self.half(1), self.minus)

    def middle(self):
        m = self.rows // 2
        right, left = (self.pos + 1) % 4, (self.pos + 3) % 4
        net, part, sent, half = self.net, self.part, self.sent, self.half
        kind = half(0).dtype
        sent(1, m, m)[...] = part(right, m, m)[...].astype(kind)
        sent(2, 0, m)[...] = part(left, 0, m)[...].astype(kind)
        net.arrived(self.ka, half(0))
        sent(1, 0, m)[...] = (part(right, 0, m)[...] + half(0)[...].astype(F32)).astype(kind)
        self.kp = net.push(sent(1, 0, self.rows), self.full(0), self.plus)
        net.arrived(self.kb, half(1))
        sent(2, m, m)[...] = (part(left, m, m)[...] + half(1)[...].astype(F32)).astype(kind)
        self.km = net.push(sent(2, 0, self.rows), self.full(1), self.minus)

    def finish(self):
        self.net.arrived(self.kp, self.full(0))
        self.net.arrived(self.km, self.full(1))
        return (self.part(self.pos, 0, self.rows)[...] + self.full(0)[...].astype(F32)
                + self.full(1)[...].astype(F32))


class AllGather:
    def __init__(self, net, slot, rows, pos, plus, minus):
        self.net, self.slot, self.rows = net, slot, rows
        self.pos, self.plus, self.minus = pos, plus, minus

    def start(self):
        own = self.slot(self.pos, 0, self.rows)
        self.kp = self.net.push(own, own, self.plus)
        self.km = self.net.push(own, own, self.minus)

    def forward(self):
        m = self.rows // 2
        right, left = (self.pos + 1) % 4, (self.pos + 3) % 4
        self.net.arrived(self.kp, self.slot(left, 0, self.rows))
        first = self.slot(left, 0, m)
        self.ka = self.net.push(first, first, self.plus)
        self.net.arrived(self.km, self.slot(right, 0, self.rows))
        second = self.slot(right, m, m)
        self.kb = self.net.push(second, second, self.minus)

    def finish(self):
        m = self.rows // 2
        far = (self.pos + 2) % 4
        self.net.arrived(self.ka, self.slot(far, 0, m))
        self.net.arrived(self.kb, self.slot(far, m, m))


def kernel(tok, cot, wg, wu, wd, lo, gt, t_out, g_out, gd_out,
           T, C, W, V, H, G, PG, PH, GU, sg, hg, fg, sh, hh, fh,
           own, give, take, sx, hx, fx, sy, ry, gs, gr, send, recv):
    gx, gy, gz = lax.axis_index("gx"), lax.axis_index("gy"), lax.axis_index("gz")
    x, z, c = gx // 2, gz, gy % 2
    yh, yl = gy // 2, gx % 2
    y = yh * 2 + yl

    def at(x, y, z, c):
        return (x * 2 + y % 2, (y // 2) * 2 + c, z)

    def span(start, size):
        return pl.ds(pl.multiple_of(start, size), size)

    ys = [at(x, (y + d) % 4, z, c) for d in (1, 2, 3)]
    xs = [at((x + d) % 4, y, z, c) for d in (1, 2, 3)]
    zp, zm = at(x, y, (z + 1) % 4, c), at(x, y, (z + 3) % 4, c)
    mate = at(x, y, z, 1 - c)
    cross = at(x, (y + 2) % 4, z, 1 - c)
    net = Net(send, recv)

    loads = [net.local(tok, T.at[gy, :, span(gx * 128, 128)]),
             net.local(cot, C.at[gy, :, span(gx * 128, 128)])]
    w_loads = [net.local(wg, W.at[:, pl.ds(0, 512)]), net.local(wu, W.at[:, pl.ds(512, 512)])]
    v_load = net.local(wd.at[span(gy * 512, 512)], V.at[:, span(gy * 256, 256)])

    barrier = pltpu.get_barrier_semaphore()
    peers = ys + xs + [zp, zm, mate, cross]
    for peer in peers:
        pl.semaphore_signal(barrier, inc=1, device_id=peer, device_id_type=MESH)
    pl.semaphore_wait(barrier, len(peers))

    waits = {}

    def need(*keys):
        for key in keys:
            if key in waits:
                waits.pop(key)()

    def gather_y(src, buf, r, n):
        rows = pl.ds(r * n, n)
        mine = buf.at[gy, rows, span(gx * 128, 128)]
        ks = [net.push(src.at[rows], mine, d) for d in ys]

        def done():
            for d, k in zip((3, 2, 1), ks):
                yy = (y + d) % 4
                net.arrived(k, buf.at[(yy // 2) * 2 + c, rows, span((x * 2 + yy % 2) * 128, 128)])
        return done

    def gather_x(buf, h, r, n):
        rows = pl.ds(r * n, n)
        mine = buf.at[h * 2 + c, rows, span(x * 256, 256)]
        ks = [net.push(mine, mine, d) for d in xs]

        def done():
            for d, k in zip((3, 2, 1), ks):
                net.arrived(k, buf.at[h * 2 + c, rows, span(((x + d) % 4) * 256, 256)])
        return done

    def share(buf, h):
        mine = buf.at[h * 2 + c]
        k = net.push(mine, mine, mate)
        return lambda: net.arrived(k, buf.at[h * 2 + 1 - c])

    chunk = [c, 1 - c, 2 + 1 - c, 2 + c]
    parts = [(i, r) for i in range(4) for r in range(PARTS[i])]
    rs_g, rs_h, ag_h, ag_g, rs_x = {}, {}, {}, {}, {}

    def ring_z(i, r, P, s, h, f):
        n = 256 // PARTS[i]
        q = n // 4
        return ReduceScatter(
            net, lambda k, a, m: P.at[i, span(r * n + k * q + a, m)],
            lambda k, a, m: s.at[i, k, pl.ds(r * q + a, m)],
            lambda k: h.at[i, k, pl.ds(r * q // 2, q // 2)],
            lambda k: f.at[i, k, pl.ds(r * q, q)], q, z, zp, zm)

    def gather_z(i, r, B):
        n = 256 // PARTS[i]
        q = n // 4
        return AllGather(net, lambda k, a, m: B.at[chunk[i], span(r * n + k * q + a, m)], q, z, zp, zm)

    def ring_x(m, o, r, n):
        return ReduceScatter(
            net, lambda k, a, l: own.at[m, o, k, pl.ds(r * n + a, l)],
            lambda k, a, l: sx.at[m, o, k, pl.ds(r * n + a, l)],
            lambda k: hx.at[m, o, k, pl.ds(r * n // 2, n // 2)],
            lambda k: fx.at[m, o, k, pl.ds(r * n, n)], n, x, xs[0], xs[2])

    for i, r in parts:
        rs_g[i, r] = ring_z(i, r, PG, sg, hg, fg)
        rs_h[i, r] = ring_z(i, r, PH, sh, hh, fh)
        ag_h[i, r] = gather_z(i, r, H)
        ag_g[i, r] = gather_z(i, r, G)
        if i in (0, 3):
            for m in range(2):
                rs_x[m, i // 3, r] = ring_x(m, i // 3, r, 256 // PARTS[i])

    def rows_of(i, r):
        n = 256 // PARTS[i]
        return pl.ds(r * n, n)

    def quarter(i, r):
        q = 64 // PARTS[i]
        return pl.ds(r * q, q)

    def all_of(copies):
        return lambda: [copy.wait() for copy in copies]

    waits["own"], waits["weights"] = all_of(loads), all_of(w_loads)

    def ty(r):
        waits["ty", r] = gather_y(tok, T, r, 256 // TPARTS)

    def tx(h, r):
        need("own", ("ty", r))
        waits["tx", h, r] = gather_x(T, h, r, 256 // TPARTS)

    def tm(h):
        need(*[("tx", h, r) for r in range(TPARTS)])
        waits["tm", h] = share(T, h)

    def cy():
        waits["cy"] = gather_y(cot, C, 0, 256)

    def cx(h):
        need("own", "cy")
        waits["cx", h] = gather_x(C, h, 0, 256)

    def cm(h):
        need(("cx", h))
        waits["cm", h] = share(C, h)

    def v():
        waits["v"] = down_share()

    def save(src, dst):
        keep.append(net.local(src, dst))

    def g1(i, r):
        need("weights")
        if i in (0, 3):
            need(*[("tx", i // 3, q) for q in ([r] if TPARTS == PARTS[i] else range(TPARTS))])
        else:
            need(("tm", i - 1))
        PG[i, rows_of(i, r)] = dot(T[chunk[i], rows_of(i, r)], W[...], ((1,), (0,)))
        rs_g[i, r].start()

    def g2(i, r):
        rs_g[i, r].middle()

    def g3(i, r):
        s = rs_g[i, r].finish()
        GU[i, quarter(i, r)] = s
        gate, up = s[:, :512], s[:, 512:]
        gather = ag_h[i, r]
        gather.slot(z, 0, gather.rows)[...] = (gate * jax.nn.sigmoid(gate) * up).astype(BF)
        gather.start()

    def g4(i, r):
        ag_h[i, r].forward()

    def h1(i, r):
        need("v", ("cx", i // 3) if i in (0, 3) else ("cm", i - 1))
        PH[i, rows_of(i, r)] = dot(C[chunk[i], rows_of(i, r)], V[...], ((1,), (1,)))
        rs_h[i, r].start()

    def h2(i, r):
        rs_h[i, r].middle()

    def h3(i, r):
        grad = rs_h[i, r].finish()
        gate, up = GU[i, quarter(i, r), :512], GU[i, quarter(i, r), 512:]
        s = jax.nn.sigmoid(gate)
        gather = ag_g[i, r]
        slot = gather.slot(z, 0, gather.rows)
        slot[:, :512] = (grad * up * s * (1.0 + gate * (1.0 - s))).astype(BF)
        slot[:, 512:] = (grad * (gate * s)).astype(BF)
        gather.start()

    def h4(i, r):
        ag_g[i, r].forward()

    took = {}

    def place(m, i, r, part):
        dst = (own.at[m, 0], give.at[m, 0], give.at[m, 1], own.at[m, 1])[i]
        rows = rows_of(i, r)
        for n in range(4):
            dst[n, rows] = part[:, n * 256:n * 256 + 256]
        if i in (1, 2):
            there = take.at[m, i - 1, :, rows]
            took[m, i - 1, r] = net.push(dst.at[:, rows], there, mate), there

    def g5(i, r):
        need("v")
        ag_h[i, r].finish()
        place(0, i, r, dot(H[chunk[i], rows_of(i, r)], V[...], ((1,), (0,))))

    def h5(i, r):
        ag_g[i, r].finish()
        place(1, i, r, dot(G[chunk[i], rows_of(i, r)], W[...], ((1,), (1,))))
        if all((h5, i, q) in ran or q == r for q in range(PARTS[i])):
            save(G.at[chunk[i]], g_out.at[chunk[i]])

    def x1(m, i, r):
        o = i // 3
        if PARTS[1 + o] == PARTS[i]:
            keys = [r]
        else:
            keys = range(PARTS[1 + o])
        for q in keys:
            if (m, o, q) in took:
                net.arrived(*took.pop((m, o, q)))
        rows = rows_of(i, r)
        for n in range(4):
            own[m, o, n, rows] += take[m, o, n, rows]
        rs_x[m, o, r].start()

    def x2(m, i, r):
        rs_x[m, i // 3, r].middle()

    ky = {(m, i // 3, r): [net.slot() for _ in range(3)] for m in range(2) for i, r in parts if i in (0, 3)}

    def y_copy(m, i, r, t, d):
        o, rows = i // 3, rows_of(i, r)
        k = ky[m, o, r][d - 1]
        return pltpu.make_async_remote_copy(
            src_ref=sy.at[m, o, t, rows], dst_ref=ry.at[m, d - 1, rows],
            send_sem=send.at[k], recv_sem=recv.at[k],
            device_id=at(x, 2 * o + t, z, c), device_id_type=MESH)

    def x3(m, i, r):
        o, rows = i // 3, rows_of(i, r)
        total = rs_x[m, o, r].finish()
        sy[m, o, 0, rows] = total[:, :128].astype(YT)
        sy[m, o, 1, rows] = total[:, 128:].astype(YT)
        for t in range(2):
            for d in (1, 2, 3):
                @pl.when((y + d) % 4 == 2 * o + t)
                def _():
                    y_copy(m, i, r, t, d).start()

    def y_sent(m, i, r):
        for t in range(2):
            for d in (1, 2, 3):
                @pl.when((y + d) % 4 == 2 * (i // 3) + t)
                def _():
                    y_copy(m, i, r, t, d).wait_send()

    def y_all(m):
        for i, r in parts:
            if i in (0, 3):
                @pl.when(yh == i // 3)
                def _():
                    rows = rows_of(i, r)
                    total = sy[m, i // 3, yl, rows].astype(F32)
                    for d in (1, 2, 3):
                        net.arrived(ky[m, i // 3, r][d - 1], ry.at[m, d - 1, rows])
                        total += ry[m, d - 1, rows].astype(F32)
                    (lo, gt)[m][rows] = total.astype(BF)

    others = [((1 - yh) * 2 + c, ys[1]), ((1 - yh) * 2 + 1 - c, cross), (yh * 2 + 1 - c, mate)]
    gk = []

    def down_grad():
        need(("cx", 0), ("cx", 1), ("cm", 0), ("cm", 1))
        part = dot(H[...].reshape(1024, 512), C[...].reshape(1024, 1024), ((0,), (0,))).astype(BF)
        for g in range(4):
            gs[g] = part[:, g * 256:g * 256 + 256]
        gk.extend((net.push(gs.at[g], gr.at[gy], device), g) for g, device in others)
        gr[gy] = gs[gy]

    def down_done():
        for k, g in gk:
            net.arrived(k, gr.at[g])
        save(gr, gd_out)

    def down_share():
        dst = V.at[:, span(gy * 256, 256)]
        ks = [(net.push(wd.at[span(g * 512, 512)], dst, device), g) for g, device in others]

        def done():
            for k, g in ks:
                net.arrived(k, V.at[:, span(g * 256, 256)])
            v_load.wait()
        return done

    keep, ran = [], set()

    steps = [
        (ty, 0), (ty, 1), (cy,), (tx, 1, 0), (tx, 0, 0), (tx, 0, 1), (tx, 1, 1), (g1, 3, 0),
        (g1, 0, 0), (g2, 3, 0), (g1, 0, 1), (g2, 0, 0), (g3, 3, 0), (v,), (tm, 1), (g2, 0, 1),
        (tm, 0), (g1, 3, 1), (cx, 1), (g3, 0, 0), (g1, 2, 0), (g1, 1, 0), (g4, 0, 0), (cx, 0),
        (g2, 3, 1), (g2, 2, 0), (g3, 3, 1), (g2, 1, 0), (cm, 1), (g3, 2, 0), (g3, 0, 1), (g4, 3, 1),
        (cm, 0), (h1, 2, 0), (g4, 3, 0), (g3, 1, 0), (g4, 2, 0), (h1, 3, 0), (h2, 2, 0), (h1, 0, 1),
        (h1, 1, 0), (g4, 1, 0), (h1, 0, 0), (g5, 3, 0), (g5, 2, 0), (g4, 0, 1), (h2, 3, 0),
        (h3, 2, 0), (h2, 1, 0), (g5, 1, 0), (g5, 0, 0), (h1, 3, 1), (x1, 0, 3, 0), (h2, 0, 1),
        (g5, 0, 1), (h4, 2, 0), (x1, 0, 0, 0), (h3, 3, 0), (g5, 3, 1), (x1, 0, 3, 1), (x1, 0, 0, 1),
        (h3, 1, 0), (down_grad,), (h5, 2, 0), (h4, 3, 0), (h2, 3, 1), (x2, 0, 0, 1), (x2, 0, 0, 0),
        (h3, 0, 1), (x2, 0, 3, 1), (h2, 0, 0), (h4, 1, 0), (h5, 3, 0), (h3, 3, 1), (x1, 1, 3, 0),
        (h3, 0, 0), (h4, 0, 1), (x3, 0, 0, 0), (h5, 1, 0), (x2, 0, 3, 0), (x3, 0, 0, 1), (h4, 3, 1),
        (x3, 0, 3, 1), (x2, 1, 3, 0), (h4, 0, 0), (h5, 0, 1), (x1, 1, 0, 1), (h5, 3, 1),
        (x1, 1, 3, 1), (h5, 0, 0), (x1, 1, 0, 0), (x3, 0, 3, 0), (x2, 1, 0, 1), (x2, 1, 3, 1),
        (x3, 1, 3, 0), (down_done,), (x2, 1, 0, 0), (x3, 1, 0, 1), (y_all, 0), (x3, 1, 3, 1),
        (x3, 1, 0, 0), (y_all, 1),
    ]
    for f, *args in steps:
        f(*args)
        ran.add((f, *args))
        if f is tm and len([s for s in ran if s[0] is tm]) == 2:
            need(("tm", 0), ("tm", 1))
            save(T, t_out)
    for copy in keep:
        copy.wait()
    for m in range(2):
        for i, r in parts:
            if i in (0, 3):
                y_sent(m, i, r)
    net.drain()


def local(tok, cot, wg, wu, wd):
    any_, vmem = pl.BlockSpec(memory_space=pl.ANY), pl.BlockSpec(memory_space=pltpu.VMEM)
    S = jax.ShapeDtypeStruct
    scratch = [
        pltpu.VMEM((4, 256, 1024), BF),
        pltpu.VMEM((4, 256, 1024), BF),
        pltpu.VMEM((1024, 1024), BF),
        pltpu.VMEM((512, 1024), BF),
        pltpu.VMEM((4, 256, 512), BF),
        pltpu.VMEM((4, 256, 1024), BF),
        pltpu.VMEM((4, 256, 1024), F32),
        pltpu.VMEM((4, 256, 512), F32),
        pltpu.VMEM((4, 64, 1024), F32),
        pltpu.VMEM((4, 3, 64, 1024), BF),
        pltpu.VMEM((4, 2, 32, 1024), BF),
        pltpu.VMEM((4, 2, 64, 1024), BF),
        pltpu.VMEM((4, 3, 64, 512), BF),
        pltpu.VMEM((4, 2, 32, 512), BF),
        pltpu.VMEM((4, 2, 64, 512), BF),
        pltpu.VMEM((2, 2, 4, 256, 256), F32),
        pltpu.VMEM((2, 2, 4, 256, 256), F32),
        pltpu.VMEM((2, 2, 4, 256, 256), F32),
        pltpu.VMEM((2, 2, 3, 256, 256), XT),
        pltpu.VMEM((2, 2, 2, 128, 256), XT),
        pltpu.VMEM((2, 2, 2, 256, 256), XT),
        pltpu.VMEM((2, 2, 2, 256, 128), YT),
        pltpu.VMEM((2, 3, 256, 128), YT),
        pltpu.VMEM((4, 512, 256), BF),
        pltpu.VMEM((4, 512, 256), BF),
        pltpu.SemaphoreType.DMA((NSEM,)),
        pltpu.SemaphoreType.DMA((NSEM,)),
    ]
    lo, gt, t_all, g_all, gd = pl.pallas_call(
        kernel,
        out_shape=[S((256, 128), BF), S((256, 128), BF), S((4, 256, 1024), BF),
                   S((4, 256, 1024), BF), S((4, 512, 256), BF)],
        in_specs=[any_] * 5,
        out_specs=[vmem, vmem, any_, any_, any_],
        scratch_shapes=scratch,
        compiler_params=pltpu.CompilerParams(
            collective_id=0, has_side_effects=True, vmem_limit_bytes=56 << 20),
        cost_estimate=pl.CostEstimate(flops=8_000_000_000, bytes_accessed=10_000_000, transcendentals=600_000),
        name="layer",
    )(tok, cot, wg, wu, wd)
    return weight_grads(lo, gt, t_all.reshape(1024, 1024), g_all.reshape(1024, 1024), gd.reshape(2048, 256))


def weight_grads_kernel(lo, gt, t_in, g_in, gd_in, lo_out, gt_out, gg_out, gu_out, gd_out, T, G, D, gg, gu, gd, sems):
    count = [0]

    def copy(src, dst):
        made = pltpu.make_async_copy(src, dst, sems.at[count[0]])
        count[0] += 1
        made.start()
        return made

    blocks = [pl.ds(n * 256, 256) for n in range(4)]
    first = [copy(g_in.at[rows], G.at[rows]) for rows in blocks]
    t_loads = [copy(t_in.at[:, cols], T.at[:, cols]) for cols in blocks]
    d_loads = [copy(gd_in.at[pl.ds(n * 1024, 1024)], D.at[pl.ds(n * 1024, 1024)]) for n in range(2)]
    small = [copy(lo, lo_out), copy(gt, gt_out)]
    for load in first:
        load.wait()
    stores = []
    for n in range(4):
        rows = blocks[n]
        t_loads[n].wait()
        part = dot(T[:, rows], G[...], ((0,), (0,)))
        gg[rows] = part[:, :512]
        stores.append(copy(gg.at[rows], gg_out.at[rows]))
        gu[rows] = part[:, 512:]
        stores.append(copy(gu.at[rows], gu_out.at[rows]))
        if n < 2:
            rows = pl.ds(n * 1024, 1024)
            d_loads[n].wait()
            gd[rows] = D[rows].astype(F32)
            stores.append(copy(gd.at[rows], gd_out.at[rows]))
    for made in stores + small:
        made.wait()


def weight_grads(lo, gt, t_all, g_all, gd):
    any_ = pl.BlockSpec(memory_space=pl.ANY)
    S = jax.ShapeDtypeStruct
    return pl.pallas_call(
        weight_grads_kernel,
        out_shape=[S((256, 128), BF), S((256, 128), BF), S((1024, 512), F32), S((1024, 512), F32),
                   S((2048, 256), F32)],
        in_specs=[any_] * 5,
        out_specs=[any_] * 5,
        scratch_shapes=[
            pltpu.VMEM((1024, 1024), BF), pltpu.VMEM((1024, 1024), BF), pltpu.VMEM((2048, 256), BF),
            pltpu.VMEM((1024, 512), F32), pltpu.VMEM((1024, 512), F32), pltpu.VMEM((2048, 256), F32),
            pltpu.SemaphoreType.DMA((24,))],
        compiler_params=pltpu.CompilerParams(vmem_limit_bytes=60 << 20),
        cost_estimate=pl.CostEstimate(flops=2_200_000_000, bytes_accessed=12_000_000, transcendentals=0),
        name="weight_grads",
    )(lo, gt, t_all, g_all, gd)


def solution(mesh):
    ins = (P("gy", ("gz", "gx")), P("gy", ("gz", "gx")), P("gz", ("gx", "gy")),
           P("gz", ("gx", "gy")), P("gx", ("gz", "gy")))
    outs = (P("gy", ("gz", "gx")), P("gy", ("gz", "gx")), P("gz", ("gx", "gy")),
            P("gz", ("gx", "gy")), P("gx", ("gz", "gy")))
    return jax.shard_map(local, mesh=mesh, in_specs=ins, out_specs=outs, check_vma=False)
```

time: 653 us -> 102 us (0.16)
  waiting for transfers between devices: 529 us -> 0 us
  Pallas kernels: 0 us -> 101 us
  blocking collectives: 53.4 us -> 0 us
  matrix products: 41.2 us -> 0 us
  between operations: 14 us -> 0.8 us
  local copies, waits for them, and re-layouts: 8.07 us -> 0 us
    reduce_scatter x8 -> x0, waiting for transfers between devices: 389 us -> none  [the longest x1 78.8 us: local(): lax.psum_scatter(up_wpart, 'gy', scatter_dimension=1, tiled=True)]
    all_gather x6 -> x0, waiting for transfers between devices: 136 us -> none  [the longest x1 34.9 us: local(): lax.all_gather(gate_weight, 'gy', axis=1, tiled=True)]
    pallas_call x0 -> x2, Pallas kernels: none -> 101 us  [the longest x1 95.5 us: local(): pl.pallas_call(kernel, out_shape=[S((256, 128), BF), S((256, 128), BF), S...]
    all_gather x2 -> x0, blocking collectives: 53.4 us -> none  [the longest x1 26.9 us: local(): cot_cols = lax.all_gather(cotangent, 'gx', axis=1, tiled=True)]
    dot_general x9 -> x0, matrix products: 41.2 us -> none  [the longest x3 13.6 us: matmul_tn(): lax.dot_general(left, right, (((0,), (0,)), ((), ())), preferred_element_...]
    unnamed x10 -> x0, local copies, waits for them, and re-layouts: 8.07 us -> none
  transfers between devices with their start and end apart: 14 -> 0, of which waited for: 14 -> 0; matrix products, arithmetic and copies ran while one was open for 8% -> 0% of each run, Pallas kernels for 0% -> 0%
where the time goes in v2:
time: 102 us
  Pallas kernels  101 us (99%)
    pallas_call x1, Pallas kernels, local(): pl.pallas_call(kernel, out_shape=[S((256, 128), BF), S((256, 128), BF), S...  95.5 us
    pallas_call x1, Pallas kernels, weight_grads(): pl.pallas_call(weight_grads_kernel, out_shape=[S((256, 128), BF), S((256,...  5.83 us

profile of v2, /device:TPU:0, one launch (start us, length us, event | category | flops | bytes accessed | tf_op | source)
XLA Modules:
  0.0 102.2 jit_solution(7820370734890276501)
XLA Ops:
  0.6 95.5 %layer.1 = (bf16[256,128]{1,0:T(8,128)(2,1)}, bf16[256,128]{1,0:T(8,128)(2,1)}, bf16[4,256,1024]{2,1,0:T(8,128)(2,1)}, bf16[4,256,1024]{2,1,0:T(8,128)(2,1)}, bf16[4,512,256]{2,1,0:T(8,128)(2,1)}) custom-call(bf16[256,128]{1,0:T(8,128)(2,1)} %tok.1, bf16[256,128]{1,0:T(8,128)(2,1)} %cot.1, bf16[1024,512]{1,0:T(8,128)(2,1)} %wg.1, bf16[1024,512]{1,0:T(8,128)(2,1)} %wu.1, ...), custom_call_target="tpu_custom_call" | custom-call | flops 8000000000 | bytes 10000000 | tf_op jit(solution)/shard_map/layer/pallas_call | solution.py:468
  96.2 5.8 %weight_grads.1 = (bf16[256,128]{1,0:T(8,128)(2,1)}, bf16[256,128]{1,0:T(8,128)(2,1)}, f32[1024,512]{1,0:T(8,128)}, f32[1024,512]{1,0:T(8,128)}, f32[2048,256]{1,0:T(8,128)}) custom-call(bf16[256,128]{1,0:T(8,128)(2,1)} %get-tuple-element.10.lo, bf16[256,128]{1,0:T(8,128)(2,1)} %get-tuple-element.11.gt, bf16[1024,1024]{1,0:T(8,128)(2,1)} %bitcast.3, ...), custom_call_target="tpu_custom_call" | custom-call | flops 2200000000 | bytes 12000000 | tf_op jit(solution)/shard_map/weight_grads/pallas_call | solution.py:520

commit v3 on v2

--- a/solution.py
+++ b/solution.py
@@ -8,7 +8,7 @@
 MESH = pl.DeviceIdType.MESH
 BF, F32 = jnp.bfloat16, jnp.float32
 XT = jnp.bfloat16
-YT = jnp.float32
+YT = jnp.bfloat16
 NSEM = 256
 PARTS = (2, 1, 1, 2)
 TPARTS = 2
@@ -112,7 +112,7 @@
 
 def kernel(tok, cot, wg, wu, wd, lo, gt, t_out, g_out, gd_out,
            T, C, W, V, H, G, PG, PH, GU, sg, hg, fg, sh, hh, fh,
-           own, give, take, sx, hx, fx, sy, ry, gs, gr, send, recv):
+           own, give, take, sx, hx, fx, sy, ry, mine, gs, gr, send, recv):
     gx, gy, gz = lax.axis_index("gx"), lax.axis_index("gy"), lax.axis_index("gz")
     x, z, c = gx // 2, gz, gy % 2
     yh, yl = gy // 2, gx % 2
@@ -348,6 +348,14 @@
         total = rs_x[m, o, r].finish()
         sy[m, o, 0, rows] = total[:, :128].astype(YT)
         sy[m, o, 1, rows] = total[:, 128:].astype(YT)
+
+        @pl.when(y == 2 * o)
+        def _():
+            mine[m, rows] = total[:, :128]
+
+        @pl.when(y == 2 * o + 1)
+        def _():
+            mine[m, rows] = total[:, 128:]
         for t in range(2):
             for d in (1, 2, 3):
                 @pl.when((y + d) % 4 == 2 * o + t)
@@ -367,7 +375,7 @@
                 @pl.when(yh == i // 3)
                 def _():
                     rows = rows_of(i, r)
-                    total = sy[m, i // 3, yl, rows].astype(F32)
+                    total = mine[m, rows]
                     for d in (1, 2, 3):
                         net.arrived(ky[m, i // 3, r][d - 1], ry.at[m, d - 1, rows])
                         total += ry[m, d - 1, rows].astype(F32)
@@ -402,21 +410,21 @@
     keep, ran = [], set()
 
     steps = [
-        (ty, 0), (ty, 1), (cy,), (tx, 1, 0), (tx, 0, 0), (tx, 0, 1), (tx, 1, 1), (g1, 3, 0),
-        (g1, 0, 0), (g2, 3, 0), (g1, 0, 1), (g2, 0, 0), (g3, 3, 0), (v,), (tm, 1), (g2, 0, 1),
-        (tm, 0), (g1, 3, 1), (cx, 1), (g3, 0, 0), (g1, 2, 0), (g1, 1, 0), (g4, 0, 0), (cx, 0),
-        (g2, 3, 1), (g2, 2, 0), (g3, 3, 1), (g2, 1, 0), (cm, 1), (g3, 2, 0), (g3, 0, 1), (g4, 3, 1),
-        (cm, 0), (h1, 2, 0), (g4, 3, 0), (g3, 1, 0), (g4, 2, 0), (h1, 3, 0), (h2, 2, 0), (h1, 0, 1),
-        (h1, 1, 0), (g4, 1, 0), (h1, 0, 0), (g5, 3, 0), (g5, 2, 0), (g4, 0, 1), (h2, 3, 0),
-        (h3, 2, 0), (h2, 1, 0), (g5, 1, 0), (g5, 0, 0), (h1, 3, 1), (x1, 0, 3, 0), (h2, 0, 1),
-        (g5, 0, 1), (h4, 2, 0), (x1, 0, 0, 0), (h3, 3, 0), (g5, 3, 1), (x1, 0, 3, 1), (x1, 0, 0, 1),
-        (h3, 1, 0), (down_grad,), (h5, 2, 0), (h4, 3, 0), (h2, 3, 1), (x2, 0, 0, 1), (x2, 0, 0, 0),
-        (h3, 0, 1), (x2, 0, 3, 1), (h2, 0, 0), (h4, 1, 0), (h5, 3, 0), (h3, 3, 1), (x1, 1, 3, 0),
-        (h3, 0, 0), (h4, 0, 1), (x3, 0, 0, 0), (h5, 1, 0), (x2, 0, 3, 0), (x3, 0, 0, 1), (h4, 3, 1),
-        (x3, 0, 3, 1), (x2, 1, 3, 0), (h4, 0, 0), (h5, 0, 1), (x1, 1, 0, 1), (h5, 3, 1),
-        (x1, 1, 3, 1), (h5, 0, 0), (x1, 1, 0, 0), (x3, 0, 3, 0), (x2, 1, 0, 1), (x2, 1, 3, 1),
-        (x3, 1, 3, 0), (down_done,), (x2, 1, 0, 0), (x3, 1, 0, 1), (y_all, 0), (x3, 1, 3, 1),
-        (x3, 1, 0, 0), (y_all, 1),
+        (ty, 0), (ty, 1), (cy,), (tx, 1, 0), (tx, 1, 1), (g1, 3, 0), (v,), (tx, 0, 1), (tm, 1),
+        (g1, 3, 1), (tx, 0, 0), (g2, 3, 0), (cx, 0), (g1, 2, 0), (cx, 1), (g2, 3, 1), (g3, 3, 0),
+        (g1, 0, 1), (tm, 0), (g2, 2, 0), (g3, 3, 1), (g1, 1, 0), (g2, 0, 1), (h1, 0, 0), (cm, 0),
+        (g3, 2, 0), (g1, 0, 0), (g4, 3, 0), (h1, 1, 0), (g2, 1, 0), (h1, 0, 1), (g4, 2, 0),
+        (g2, 0, 0), (g3, 0, 1), (h1, 3, 1), (g3, 1, 0), (g4, 3, 1), (cm, 1), (g5, 2, 0), (h2, 0, 0),
+        (g3, 0, 0), (h1, 2, 0), (g5, 3, 0), (x1, 0, 3, 0), (g4, 0, 1), (h2, 0, 1), (h2, 1, 0),
+        (g4, 0, 0), (g5, 3, 1), (x2, 0, 3, 0), (g4, 1, 0), (h2, 2, 0), (h2, 3, 1), (h3, 1, 0),
+        (g5, 1, 0), (x3, 0, 3, 0), (g5, 0, 0), (x1, 0, 3, 1), (h3, 0, 0), (g5, 0, 1), (h1, 3, 0),
+        (h3, 2, 0), (x1, 0, 0, 0), (x1, 0, 0, 1), (down_grad,), (h4, 1, 0), (x2, 0, 3, 1),
+        (x2, 0, 0, 0), (h3, 0, 1), (h2, 3, 0), (h4, 0, 0), (h4, 2, 0), (h3, 3, 1), (h5, 1, 0),
+        (x2, 0, 0, 1), (h4, 0, 1), (h5, 0, 0), (h3, 3, 0), (x1, 1, 0, 0), (h5, 2, 0), (h4, 3, 1),
+        (h5, 0, 1), (x1, 1, 0, 1), (x3, 0, 0, 0), (h4, 3, 0), (x2, 1, 0, 0), (x3, 0, 3, 1),
+        (h5, 3, 1), (x1, 1, 3, 1), (x3, 0, 0, 1), (x2, 1, 0, 1), (h5, 3, 0), (x1, 1, 3, 0),
+        (x3, 1, 0, 0), (x2, 1, 3, 1), (x2, 1, 3, 0), (down_done,), (x3, 1, 0, 1), (x3, 1, 3, 1),
+        (y_all, 0), (x3, 1, 3, 0), (y_all, 1),
     ]
     for f, *args in steps:
         f(*args)
@@ -460,6 +468,7 @@
         pltpu.VMEM((2, 2, 2, 256, 256), XT),
         pltpu.VMEM((2, 2, 2, 256, 128), YT),
         pltpu.VMEM((2, 3, 256, 128), YT),
+        pltpu.VMEM((2, 256, 128), F32),
         pltpu.VMEM((4, 512, 256), BF),
         pltpu.VMEM((4, 512, 256), BF),
         pltpu.SemaphoreType.DMA((NSEM,)),

time: 102 us -> 97.7 us (0.958)
  Pallas kernels: 101 us -> 96.1 us
    pallas_call x1, Pallas kernels: 95.5 us -> 90.3 us  [local(): pl.pallas_call(kernel, out_shape=[S((256, 128), BF), S((256, 128), BF), S...]
where the time goes in v3:
time: 97.7 us; the launch traced here: 96.9 us
  Pallas kernels  96.1 us (98%)
    pallas_call x1, Pallas kernels, local(): pl.pallas_call(kernel, out_shape=[S((256, 128), BF), S((256, 128), BF), S...  90.3 us
    pallas_call x1, Pallas kernels, weight_grads(): pl.pallas_call(weight_grads_kernel, out_shape=[S((256, 128), BF), S((256,...  5.83 us

profile of v3, /device:TPU:0, one launch (start us, length us, event | category | flops | bytes accessed | tf_op | source)
XLA Modules:
  0.0 96.9 jit_solution(7436048415345973738)
XLA Ops:
  0.6 90.3 %layer.1 = (bf16[256,128]{1,0:T(8,128)(2,1)}, bf16[256,128]{1,0:T(8,128)(2,1)}, bf16[4,256,1024]{2,1,0:T(8,128)(2,1)}, bf16[4,256,1024]{2,1,0:T(8,128)(2,1)}, bf16[4,512,256]{2,1,0:T(8,128)(2,1)}) custom-call(bf16[256,128]{1,0:T(8,128)(2,1)} %tok.1, bf16[256,128]{1,0:T(8,128)(2,1)} %cot.1, bf16[1024,512]{1,0:T(8,128)(2,1)} %wg.1, bf16[1024,512]{1,0:T(8,128)(2,1)} %wu.1, ...), custom_call_target="tpu_custom_call" | custom-call | flops 8000000000 | bytes 10000000 | tf_op jit(solution)/shard_map/layer/pallas_call | solution.py:477
  90.9 5.8 %weight_grads.1 = (bf16[256,128]{1,0:T(8,128)(2,1)}, bf16[256,128]{1,0:T(8,128)(2,1)}, f32[1024,512]{1,0:T(8,128)}, f32[1024,512]{1,0:T(8,128)}, f32[2048,256]{1,0:T(8,128)}) custom-call(bf16[256,128]{1,0:T(8,128)(2,1)} %get-tuple-element.10.lo, bf16[256,128]{1,0:T(8,128)(2,1)} %get-tuple-element.11.gt, bf16[1024,1024]{1,0:T(8,128)(2,1)} %bitcast.3, ...), custom_call_target="tpu_custom_call" | custom-call | flops 2200000000 | bytes 12000000 | tf_op jit(solution)/shard_map/weight_grads/pallas_call | solution.py:529

commit v4 on v3

--- a/solution.py
+++ b/solution.py
@@ -11,6 +11,8 @@
 YT = jnp.bfloat16
 NSEM = 256
 PARTS = (2, 1, 1, 2)
+DIRECT_Z = (3,)
+DIRECT_X = ((1, 3),)
 TPARTS = 2
 
 
@@ -83,6 +85,39 @@
                 + self.full(1)[...].astype(F32))
 
 
+class DirectScatter:
+    def __init__(self, net, part, sent, full, rows, pos, devices):
+        self.net, self.part, self.sent, self.full = net, part, sent, full
+        self.rows, self.pos, self.devices = rows, pos, devices
+
+    def start(self):
+        self.ks = []
+        for d in (1, 3, 2):
+            out = self.sent(d - 1, 0, self.rows)
+            out[...] = self.part((self.pos + d) % 4, 0, self.rows)[...].astype(out.dtype)
+            self.ks.append((self.net.push(out, self.full(d - 1), self.devices[d - 1]), d - 1))
+
+    def finish(self):
+        total = self.part(self.pos, 0, self.rows)[...]
+        for k, n in self.ks:
+            self.net.arrived(k, self.full(n))
+            total += self.full(n)[...].astype(F32)
+        return total
+
+
+class DirectGather:
+    def __init__(self, net, slot, rows, pos, devices):
+        self.net, self.slot, self.rows, self.pos, self.devices = net, slot, rows, pos, devices
+
+    def start(self):
+        own = self.slot(self.pos, 0, self.rows)
+        self.ks = [(self.net.push(own, own, self.devices[d - 1]), d) for d in (1, 3, 2)]
+
+    def finish(self):
+        for k, d in self.ks:
+            self.net.arrived(k, self.slot((self.pos + 4 - d) % 4, 0, self.rows))
+
+
 class AllGather:
     def __init__(self, net, slot, rows, pos, plus, minus):
         self.net, self.slot, self.rows = net, slot, rows
@@ -110,9 +145,9 @@
         self.net.arrived(self.kb, self.slot(far, m, m))
 
 
-def kernel(tok, cot, wg, wu, wd, lo, gt, t_out, g_out, gd_out,
+def kernel(tok, cot, wg, wu, wd, lo, gt, w_out, gd_out,
            T, C, W, V, H, G, PG, PH, GU, sg, hg, fg, sh, hh, fh,
-           own, give, take, sx, hx, fx, sy, ry, mine, gs, gr, send, recv):
+           own, give, take, sx, hx, fx, sy, ry, mine, gs, gr, ww, send, recv):
     gx, gy, gz = lax.axis_index("gx"), lax.axis_index("gy"), lax.axis_index("gz")
     x, z, c = gx // 2, gz, gy % 2
     yh, yl = gy // 2, gx % 2
@@ -126,7 +161,8 @@
 
     ys = [at(x, (y + d) % 4, z, c) for d in (1, 2, 3)]
     xs = [at((x + d) % 4, y, z, c) for d in (1, 2, 3)]
-    zp, zm = at(x, y, (z + 1) % 4, c), at(x, y, (z + 3) % 4, c)
+    zs = [at(x, y, (z + d) % 4, c) for d in (1, 2, 3)]
+    zp, zm = zs[0], zs[2]
     mate = at(x, y, z, 1 - c)
     cross = at(x, (y + 2) % 4, z, 1 - c)
     net = Net(send, recv)
@@ -137,7 +173,7 @@
     v_load = net.local(wd.at[span(gy * 512, 512)], V.at[:, span(gy * 256, 256)])
 
     barrier = pltpu.get_barrier_semaphore()
-    peers = ys + xs + [zp, zm, mate, cross]
+    peers = ys + xs + zs + [mate, cross]
     for peer in peers:
         pl.semaphore_signal(barrier, inc=1, device_id=peer, device_id_type=MESH)
     pl.semaphore_wait(barrier, len(peers))
@@ -191,9 +227,19 @@
     def gather_z(i, r, B):
         n = 256 // PARTS[i]
         q = n // 4
-        return AllGather(net, lambda k, a, m: B.at[chunk[i], span(r * n + k * q + a, m)], q, z, zp, zm)
+
+        def slot(k, a, m):
+            return B.at[chunk[i], span(r * n + k * q + a, m)]
+        if B is G and i in DIRECT_Z:
+            return DirectGather(net, slot, q, z, zs)
+        return AllGather(net, slot, q, z, zp, zm)
 
     def ring_x(m, o, r, n):
+        if (m, 3 * o) in DIRECT_X:
+            return DirectScatter(
+                net, lambda k, a, l: own.at[m, o, k, pl.ds(r * n + a, l)],
+                lambda k, a, l: sx.at[m, o, k, pl.ds(r * n + a, l)],
+                lambda k: fx.at[m, o, k, pl.ds(r * n, n)], n, x, xs)
         return ReduceScatter(
             net, lambda k, a, l: own.at[m, o, k, pl.ds(r * n + a, l)],
             lambda k, a, l: sx.at[m, o, k, pl.ds(r * n + a, l)],
@@ -313,8 +359,11 @@
     def h5(i, r):
         ag_g[i, r].finish()
         place(1, i, r, dot(G[chunk[i], rows_of(i, r)], W[...], ((1,), (1,))))
-        if all((h5, i, q) in ran or q == r for q in range(PARTS[i])):
-            save(G.at[chunk[i]], g_out.at[chunk[i]])
+
+    def weight_grad(q):
+        cols = pl.ds(q * 256, 256)
+        ww[q] = dot(T[:, :, cols].reshape(1024, 256), G[...].reshape(1024, 1024), ((0,), (0,))).astype(BF)
+        save(ww.at[q], w_out.at[q])
 
     def x1(m, i, r):
         o = i // 3
@@ -407,31 +456,27 @@
             v_load.wait()
         return done
 
-    keep, ran = [], set()
+    keep = []
 
     steps = [
-        (ty, 0), (ty, 1), (cy,), (tx, 1, 0), (tx, 1, 1), (g1, 3, 0), (v,), (tx, 0, 1), (tm, 1),
-        (g1, 3, 1), (tx, 0, 0), (g2, 3, 0), (cx, 0), (g1, 2, 0), (cx, 1), (g2, 3, 1), (g3, 3, 0),
-        (g1, 0, 1), (tm, 0), (g2, 2, 0), (g3, 3, 1), (g1, 1, 0), (g2, 0, 1), (h1, 0, 0), (cm, 0),
-        (g3, 2, 0), (g1, 0, 0), (g4, 3, 0), (h1, 1, 0), (g2, 1, 0), (h1, 0, 1), (g4, 2, 0),
-        (g2, 0, 0), (g3, 0, 1), (h1, 3, 1), (g3, 1, 0), (g4, 3, 1), (cm, 1), (g5, 2, 0), (h2, 0, 0),
-        (g3, 0, 0), (h1, 2, 0), (g5, 3, 0), (x1, 0, 3, 0), (g4, 0, 1), (h2, 0, 1), (h2, 1, 0),
-        (g4, 0, 0), (g5, 3, 1), (x2, 0, 3, 0), (g4, 1, 0), (h2, 2, 0), (h2, 3, 1), (h3, 1, 0),
-        (g5, 1, 0), (x3, 0, 3, 0), (g5, 0, 0), (x1, 0, 3, 1), (h3, 0, 0), (g5, 0, 1), (h1, 3, 0),
-        (h3, 2, 0), (x1, 0, 0, 0), (x1, 0, 0, 1), (down_grad,), (h4, 1, 0), (x2, 0, 3, 1),
-        (x2, 0, 0, 0), (h3, 0, 1), (h2, 3, 0), (h4, 0, 0), (h4, 2, 0), (h3, 3, 1), (h5, 1, 0),
-        (x2, 0, 0, 1), (h4, 0, 1), (h5, 0, 0), (h3, 3, 0), (x1, 1, 0, 0), (h5, 2, 0), (h4, 3, 1),
-        (h5, 0, 1), (x1, 1, 0, 1), (x3, 0, 0, 0), (h4, 3, 0), (x2, 1, 0, 0), (x3, 0, 3, 1),
-        (h5, 3, 1), (x1, 1, 3, 1), (x3, 0, 0, 1), (x2, 1, 0, 1), (h5, 3, 0), (x1, 1, 3, 0),
-        (x3, 1, 0, 0), (x2, 1, 3, 1), (x2, 1, 3, 0), (down_done,), (x3, 1, 0, 1), (x3, 1, 3, 1),
-        (y_all, 0), (x3, 1, 3, 0), (y_all, 1),
+        (ty, 0), (ty, 1), (tx, 1, 0), (cy,), (v,), (tx, 1, 1), (g1, 3, 0), (tx, 0, 1), (tm, 1),
+        (g1, 3, 1), (g2, 3, 0), (tx, 0, 0), (g1, 2, 0), (g1, 0, 1), (g2, 3, 1), (g3, 3, 0), (cx, 0),
+        (g2, 2, 0), (g3, 3, 1), (tm, 0), (cx, 1), (g1, 0, 0), (g2, 0, 1), (g1, 1, 0), (g3, 2, 0),
+        (g2, 0, 0), (g4, 3, 1), (g4, 3, 0), (cm, 0), (g2, 1, 0), (g3, 0, 0), (h1, 0, 1), (g3, 0, 1),
+        (g5, 3, 1), (h1, 0, 0), (cm, 1), (h1, 1, 0), (g3, 1, 0), (g4, 2, 0), (h1, 2, 0), (g4, 0, 1),
+        (g5, 3, 0), (h2, 0, 1), (h2, 1, 0), (g4, 1, 0), (g5, 2, 0), (h2, 0, 0), (g4, 0, 0),
+        (h2, 2, 0), (g5, 0, 1), (h1, 3, 1), (h3, 1, 0), (g5, 1, 0), (h3, 0, 1), (g5, 0, 0),
+        (h3, 0, 0), (x1, 0, 3, 0), (x1, 0, 0, 1), (down_grad,), (h4, 1, 0), (x1, 0, 3, 1),
+        (x1, 0, 0, 0), (h3, 2, 0), (x2, 0, 3, 0), (h1, 3, 0), (h4, 0, 0), (x2, 0, 0, 1), (h2, 3, 1),
+        (h4, 0, 1), (x2, 0, 3, 1), (x2, 0, 0, 0), (h5, 1, 0), (x3, 0, 3, 0), (h4, 2, 0),
+        (x3, 0, 0, 1), (h2, 3, 0), (h5, 0, 0), (h3, 3, 1), (x1, 1, 0, 0), (h5, 0, 1), (x1, 1, 0, 1),
+        (h5, 2, 0), (h3, 3, 0), (x2, 1, 0, 0), (x3, 0, 3, 1), (x3, 0, 0, 0), (x2, 1, 0, 1),
+        (h5, 3, 1), (x1, 1, 3, 1), (down_done,), (x3, 1, 0, 0), (h5, 3, 0), (x1, 1, 3, 0),
+        (weight_grad, 2), (x3, 1, 0, 1), (weight_grad, 3), (x3, 1, 3, 1), (x3, 1, 3, 0),
+        (weight_grad, 0), (y_all, 0), (weight_grad, 1), (y_all, 1),
     ]
     for f, *args in steps:
         f(*args)
-        ran.add((f, *args))
-        if f is tm and len([s for s in ran if s[0] is tm]) == 2:
-            need(("tm", 0), ("tm", 1))
-            save(T, t_out)
     for copy in keep:
         copy.wait()
     for m in range(2):
@@ -465,31 +510,32 @@
         pltpu.VMEM((2, 2, 4, 256, 256), F32),
         pltpu.VMEM((2, 2, 3, 256, 256), XT),
         pltpu.VMEM((2, 2, 2, 128, 256), XT),
-        pltpu.VMEM((2, 2, 2, 256, 256), XT),
+        pltpu.VMEM((2, 2, 3, 256, 256), XT),
         pltpu.VMEM((2, 2, 2, 256, 128), YT),
         pltpu.VMEM((2, 3, 256, 128), YT),
         pltpu.VMEM((2, 256, 128), F32),
         pltpu.VMEM((4, 512, 256), BF),
         pltpu.VMEM((4, 512, 256), BF),
+        pltpu.VMEM((4, 256, 1024), BF),
         pltpu.SemaphoreType.DMA((NSEM,)),
         pltpu.SemaphoreType.DMA((NSEM,)),
     ]
-    lo, gt, t_all, g_all, gd = pl.pallas_call(
+    lo, gt, grads, gd = pl.pallas_call(
         kernel,
         out_shape=[S((256, 128), BF), S((256, 128), BF), S((4, 256, 1024), BF),
-                   S((4, 256, 1024), BF), S((4, 512, 256), BF)],
+                   S((4, 512, 256), BF)],
         in_specs=[any_] * 5,
-        out_specs=[vmem, vmem, any_, any_, any_],
+        out_specs=[vmem, vmem, any_, any_],
         scratch_shapes=scratch,
         compiler_params=pltpu.CompilerParams(
             collective_id=0, has_side_effects=True, vmem_limit_bytes=56 << 20),
         cost_estimate=pl.CostEstimate(flops=8_000_000_000, bytes_accessed=10_000_000, transcendentals=600_000),
         name="layer",
     )(tok, cot, wg, wu, wd)
-    return weight_grads(lo, gt, t_all.reshape(1024, 1024), g_all.reshape(1024, 1024), gd.reshape(2048, 256))
-
-
-def weight_grads_kernel(lo, gt, t_in, g_in, gd_in, lo_out, gt_out, gg_out, gu_out, gd_out, T, G, D, gg, gu, gd, sems):
+    return widen(lo, gt, grads.reshape(1024, 1024), gd.reshape(2048, 256))
+
+
+def widen_kernel(lo, gt, w_in, gd_in, lo_out, gt_out, gg_out, gu_out, gd_out, Wb, D, gg, gu, gd, sems):
     count = [0]
 
     def copy(src, dst):
@@ -498,48 +544,39 @@
         made.start()
         return made
 
-    blocks = [pl.ds(n * 256, 256) for n in range(4)]
-    first = [copy(g_in.at[rows], G.at[rows]) for rows in blocks]
-    t_loads = [copy(t_in.at[:, cols], T.at[:, cols]) for cols in blocks]
-    d_loads = [copy(gd_in.at[pl.ds(n * 1024, 1024)], D.at[pl.ds(n * 1024, 1024)]) for n in range(2)]
-    small = [copy(lo, lo_out), copy(gt, gt_out)]
-    for load in first:
-        load.wait()
-    stores = []
-    for n in range(4):
-        rows = blocks[n]
-        t_loads[n].wait()
-        part = dot(T[:, rows], G[...], ((0,), (0,)))
-        gg[rows] = part[:, :512]
-        stores.append(copy(gg.at[rows], gg_out.at[rows]))
-        gu[rows] = part[:, 512:]
-        stores.append(copy(gu.at[rows], gu_out.at[rows]))
-        if n < 2:
-            rows = pl.ds(n * 1024, 1024)
-            d_loads[n].wait()
-            gd[rows] = D[rows].astype(F32)
-            stores.append(copy(gd.at[rows], gd_out.at[rows]))
-    for made in stores + small:
+    blocks = [(pl.ds(n * 256, 256), pl.ds(n * 512, 512)) for n in range(4)]
+    loads = [(copy(w_in.at[a], Wb.at[a]), copy(gd_in.at[b], D.at[b])) for a, b in blocks]
+    stores = [copy(lo, lo_out), copy(gt, gt_out)]
+    for (a, b), (first, second) in zip(blocks, loads):
+        first.wait()
+        gg[a] = Wb[a, :512].astype(F32)
+        stores.append(copy(gg.at[a], gg_out.at[a]))
+        gu[a] = Wb[a, 512:].astype(F32)
+        stores.append(copy(gu.at[a], gu_out.at[a]))
+        second.wait()
+        gd[b] = D[b].astype(F32)
+        stores.append(copy(gd.at[b], gd_out.at[b]))
+    for made in stores:
         made.wait()
 
 
-def weight_grads(lo, gt, t_all, g_all, gd):
+def widen(lo, gt, grads, gd):
     any_ = pl.BlockSpec(memory_space=pl.ANY)
     S = jax.ShapeDtypeStruct
     return pl.pallas_call(
-        weight_grads_kernel,
+        widen_kernel,
         out_shape=[S((256, 128), BF), S((256, 128), BF), S((1024, 512), F32), S((1024, 512), F32),
                    S((2048, 256), F32)],
-        in_specs=[any_] * 5,
+        in_specs=[any_] * 4,
         out_specs=[any_] * 5,
         scratch_shapes=[
-            pltpu.VMEM((1024, 1024), BF), pltpu.VMEM((1024, 1024), BF), pltpu.VMEM((2048, 256), BF),
+            pltpu.VMEM((1024, 1024), BF), pltpu.VMEM((2048, 256), BF),
             pltpu.VMEM((1024, 512), F32), pltpu.VMEM((1024, 512), F32), pltpu.VMEM((2048, 256), F32),
             pltpu.SemaphoreType.DMA((24,))],
         compiler_params=pltpu.CompilerParams(vmem_limit_bytes=60 << 20),
-        cost_estimate=pl.CostEstimate(flops=2_200_000_000, bytes_accessed=12_000_000, transcendentals=0),
-        name="weight_grads",
-    )(lo, gt, t_all, g_all, gd)
+        cost_estimate=pl.CostEstimate(flops=0, bytes_accessed=9_500_000, transcendentals=0),
+        name="widen",
+    )(lo, gt, grads, gd)
 
 
 def solution(mesh):

time: 97.7 us -> 94.7 us (0.969)
  Pallas kernels: 96.1 us -> 93.8 us
    pallas_call x1, Pallas kernels: 90.3 us -> 88.5 us  [local(): pl.pallas_call(kernel, out_shape=[S((256, 128), BF), S((256, 128), BF), S...]
where the time goes in v4:
time: 94.7 us; the launch traced here: 94.6 us
  Pallas kernels  93.8 us (99%)
    pallas_call x1, Pallas kernels, local(): pl.pallas_call(kernel, out_shape=[S((256, 128), BF), S((256, 128), BF), S...  88.5 us
    pallas_call x1, Pallas kernels, widen(): pl.pallas_call(widen_kernel, out_shape=[S((256, 128), BF), S((256, 128),...  5.32 us

profile of v4, /device:TPU:0, one launch (start us, length us, event | category | flops | bytes accessed | tf_op | source)
XLA Modules:
  0.0 94.6 jit_solution(10276591745032346260)
XLA Ops:
  0.6 88.5 %layer.1 = (bf16[256,128]{1,0:T(8,128)(2,1)}, bf16[256,128]{1,0:T(8,128)(2,1)}, bf16[4,256,1024]{2,1,0:T(8,128)(2,1)}, bf16[4,512,256]{2,1,0:T(8,128)(2,1)}) custom-call(bf16[256,128]{1,0:T(8,128)(2,1)} %tok.1, bf16[256,128]{1,0:T(8,128)(2,1)} %cot.1, bf16[1024,512]{1,0:T(8,128)(2,1)} %wg.1, bf16[1024,512]{1,0:T(8,128)(2,1)} %wu.1, bf16[2048,256]{1,0:T(8,128)(2,1)} %wd.1), custom_call_target="tpu_custom_call" | custom-call | flops 8000000000 | bytes 10000000 | tf_op jit(solution)/shard_map/layer/pallas_call | solution.py:523
  89.1 5.3 %widen.1 = (bf16[256,128]{1,0:T(8,128)(2,1)}, bf16[256,128]{1,0:T(8,128)(2,1)}, f32[1024,512]{1,0:T(8,128)}, f32[1024,512]{1,0:T(8,128)}, f32[2048,256]{1,0:T(8,128)}) custom-call(bf16[256,128]{1,0:T(8,128)(2,1)} %get-tuple-element.9.lo, bf16[256,128]{1,0:T(8,128)(2,1)} %get-tuple-element.10.gt, bf16[1024,1024]{1,0:T(8,128)(2,1)} %bitcast.2, ...), custom_call_target="tpu_custom_call" | custom-call | bytes 9500000 | tf_op jit(solution)/shard_map/widen/pallas_call | solution.py:566

commit v5 on v4

--- a/solution.py
+++ b/solution.py
@@ -535,7 +535,7 @@
     return widen(lo, gt, grads.reshape(1024, 1024), gd.reshape(2048, 256))
 
 
-def widen_kernel(lo, gt, w_in, gd_in, lo_out, gt_out, gg_out, gu_out, gd_out, Wb, D, gg, gu, gd, sems):
+def widen_kernel(lo, gt, w_in, gd_in, lo_out, gt_out, gg_out, gu_out, gd_out, Wb, D, gg, gu, gd, small_buf, sems):
     count = [0]
 
     def copy(src, dst):
@@ -544,9 +544,10 @@
         made.start()
         return made
 
-    blocks = [(pl.ds(n * 256, 256), pl.ds(n * 512, 512)) for n in range(4)]
+    blocks = [(pl.ds(n * 128, 128), pl.ds(n * 256, 256)) for n in range(8)]
     loads = [(copy(w_in.at[a], Wb.at[a]), copy(gd_in.at[b], D.at[b])) for a, b in blocks]
-    stores = [copy(lo, lo_out), copy(gt, gt_out)]
+    small = [copy(lo, small_buf.at[0]), copy(gt, small_buf.at[1])]
+    stores = []
     for (a, b), (first, second) in zip(blocks, loads):
         first.wait()
         gg[a] = Wb[a, :512].astype(F32)
@@ -556,6 +557,11 @@
         second.wait()
         gd[b] = D[b].astype(F32)
         stores.append(copy(gd.at[b], gd_out.at[b]))
+        if small:
+            for made in small:
+                made.wait()
+            stores += [copy(small_buf.at[0], lo_out), copy(small_buf.at[1], gt_out)]
+            small = []
     for made in stores:
         made.wait()
 
@@ -572,7 +578,7 @@
         scratch_shapes=[
             pltpu.VMEM((1024, 1024), BF), pltpu.VMEM((2048, 256), BF),
             pltpu.VMEM((1024, 512), F32), pltpu.VMEM((1024, 512), F32), pltpu.VMEM((2048, 256), F32),
-            pltpu.SemaphoreType.DMA((24,))],
+            pltpu.VMEM((2, 256, 128), BF), pltpu.SemaphoreType.DMA((48,))],
         compiler_params=pltpu.CompilerParams(vmem_limit_bytes=60 << 20),
         cost_estimate=pl.CostEstimate(flops=0, bytes_accessed=9_500_000, transcendentals=0),
         name="widen",

time: 94.7 us -> 94.1 us (level)
  no operation moved by 1% of the time
where the time goes in v5:
time: 94.1 us; the launch traced here: 94 us
  Pallas kernels  93.2 us (99%)
    pallas_call x1, Pallas kernels, local(): pl.pallas_call(kernel, out_shape=[S((256, 128), BF), S((256, 128), BF), S...  88.5 us
    pallas_call x1, Pallas kernels, widen(): pl.pallas_call(widen_kernel, out_shape=[S((256, 128), BF), S((256, 128),...  4.73 us

profile of v5, /device:TPU:0, one launch (start us, length us, event | category | flops | bytes accessed | tf_op | source)
XLA Modules:
  0.0 94.0 jit_solution(3105859723215171030)
XLA Ops:
  0.6 88.5 %layer.1 = (bf16[256,128]{1,0:T(8,128)(2,1)}, bf16[256,128]{1,0:T(8,128)(2,1)}, bf16[4,256,1024]{2,1,0:T(8,128)(2,1)}, bf16[4,512,256]{2,1,0:T(8,128)(2,1)}) custom-call(bf16[256,128]{1,0:T(8,128)(2,1)} %tok.1, bf16[256,128]{1,0:T(8,128)(2,1)} %cot.1, bf16[1024,512]{1,0:T(8,128)(2,1)} %wg.1, bf16[1024,512]{1,0:T(8,128)(2,1)} %wu.1, bf16[2048,256]{1,0:T(8,128)(2,1)} %wd.1), custom_call_target="tpu_custom_call" | custom-call | flops 8000000000 | bytes 10000000 | tf_op jit(solution)/shard_map/layer/pallas_call | solution.py:523
  89.1 4.7 %widen.1 = (bf16[256,128]{1,0:T(8,128)(2,1)}, bf16[256,128]{1,0:T(8,128)(2,1)}, f32[1024,512]{1,0:T(8,128)}, f32[1024,512]{1,0:T(8,128)}, f32[2048,256]{1,0:T(8,128)}) custom-call(bf16[256,128]{1,0:T(8,128)(2,1)} %get-tuple-element.9.lo, bf16[256,128]{1,0:T(8,128)(2,1)} %get-tuple-element.10.gt, bf16[1024,1024]{1,0:T(8,128)(2,1)} %bitcast.2, ...), custom_call_target="tpu_custom_call" | custom-call | bytes 9500000 | tf_op jit(solution)/shard_map/widen/pallas_call | solution.py:572
